TPU v7x, 32 devices: a whole 2x2x4 slice. The times are simulated.
32 devices in a mesh: dp: 4 (over x, core), expert: 8 (over z, y).
Axes of the slice: x: 2, y: 2, z: 4, core: 2. Of those that a mesh axis runs over, the one named last changes fastest.
Arguments:
- grad_rows: bfloat16 [4, 16, 16, 3584], P('dp', 'expert'), may hold values from -6 to 6
- router_weight: float32 [4, 16, 16], P('dp', 'expert'), may hold values from 0.05 to 0.6
- send_counts: int32 [4, 16], P('dp', 'expert'), may hold values from 1 to 16, as said below
- gate_stash: bfloat16 [4, 128, 2048], P('dp', None, 'expert'), may hold values from -6 to 6
- up_stash: bfloat16 [4, 128, 2048], P('dp', None, 'expert'), may hold values from -6 to 6
- master_weight: float32 [3584, 2048], P('dp', 'expert'), may hold values from -0.1875 to 0.1875
- first_moment: float32 [3584, 2048], P('dp', 'expert'), may hold values from -18 to 18
- second_moment: float32 [3584, 2048], P('dp', 'expert'), may hold values from 10 to 100
Outputs:
- d_gate: bfloat16 [4, 128, 2048], P('dp', None, 'expert')
- d_up: bfloat16 [4, 128, 2048], P('dp', None, 'expert')
- new_master: float32 [3584, 2048], P('dp', 'expert')
- new_first: float32 [3584, 2048], P('dp', 'expert')
- new_second: float32 [3584, 2048], P('dp', 'expert')
- fresh_weight: bfloat16 [3584, 2048], P(None, 'expert')
Inputs may be any that keep to these rules, and one draw needn't show every extreme that they name: `send_counts`: in every replica one expert in flight receives exactly 16 rows from every source; the other counts are at most 8.
All inputs are finite; a program needn't handle non-finite values.
Results may differ from a plain program's by a relative error of at most 0.009.
Values may be sent and summed in bfloat16 or wider, within the bound.
No kernel may reach another device: no remote copies, remote signals or barrier semaphores. Data moves between devices by JAX's collectives and lax.ppermute only.
A program may use at most 64 MiB of HBM per device.

v0:
```python
import functools

import jax
import jax.numpy as jnp
from jax import lax
from jax.experimental import pallas as pl
from jax.experimental.pallas import tpu as pltpu
from jax.sharding import PartitionSpec as P

learning_rate = 0.01
beta_one = 0.9
beta_two = 0.95
decay_rate = 0.1
epsilon = 1e-08

bf16 = jnp.bfloat16
f32 = jnp.float32
VMEM_LIMIT = 40 * 1024 * 1024
LANES = 128


def params():
    return pltpu.CompilerParams(vmem_limit_bytes=VMEM_LIMIT)


def cost(flops, nbytes):
    return pl.CostEstimate(flops=flops, bytes_accessed=nbytes, transcendentals=0)


def take(refs, count):
    taken = refs[:count]
    del refs[:count]
    return taken


def wide(tiles):
    return tiles[0] if len(tiles) == 1 else jnp.concatenate(tiles, axis=1)


def tall(blocks):
    return blocks[0] if len(blocks) == 1 else jnp.concatenate(blocks, axis=0)


def turns(ways):
    return [0, *range(ways - 1, 0, -1)]


def seat_of(ways):
    seat = lax.axis_index("expert")
    return lax.axis_index("dp"), lax.rem(seat, ways), lax.div(seat, ways)


def scale_kernel(counts_in, router_in, rows_in, gate_in, up_in, *refs):
    hidden, outs = refs[0], refs[1:-7]
    counts, router, rows, gate, up, cut, sems = refs[-7:]
    copies = [
        pltpu.make_async_copy(source, target, sems.at[n])
        for n, (source, target) in enumerate(
            [
                (gate_in, gate),
                (up_in, up),
                (counts_in, counts),
                (router_in, router),
                (rows_in, rows),
            ]
        )
    ]
    for copy in copies:
        copy.start()
    flight, slots, width = rows.shape[1:]
    pieces = cut.shape[0]
    piece = width // pieces
    ways = hidden.shape[0]
    me, _, own = seat_of(ways)
    copies[0].wait()
    copies[1].wait()
    g = gate[0].astype(f32)
    value = (g * jax.nn.sigmoid(g) * up[0].astype(f32)).astype(bf16)
    for f in range(flight):
        for v in range(ways):
            at = (f * ways + v) * slots
            hidden[v, f] = value[at : at + slots]
    for copy in copies[2:]:
        copy.wait()
    diagonal = lax.broadcasted_iota(jnp.int32, (slots, slots), 0) == lax.broadcasted_iota(
        jnp.int32, (slots, slots), 1
    )
    row = lax.broadcasted_iota(jnp.int32, (slots, 1), 0)
    for f in range(flight):
        weight = jnp.sum(
            jnp.where(diagonal, jnp.broadcast_to(router[0, f : f + 1, :], (slots, slots)), 0.0),
            axis=1,
            keepdims=True,
        )
        live = row < counts[0, f]
        scaled = jnp.where(live, weight * rows[0, f].astype(f32), 0.0).astype(bf16)
        for i in range(pieces):
            cut[i, f] = scaled[:, i * piece : (i + 1) * piece]
    for n, out in enumerate(outs):
        for dc in range(2):
            out[dc] = cut[me ^ (n % (pieces // 2) * 2 + dc), own ^ (n // (pieces // 2))]


def fetch_kernel(after, *refs):
    del after
    sems = refs[6]
    copies = [pltpu.make_async_copy(refs[n], refs[3 + n], sems.at[n]) for n in range(3)]
    for copy in copies:
        copy.start()
    for copy in copies:
        copy.wait()


def share_kernel(order, *refs):
    for n, block in zip(order, refs):
        refs[-1][n] = block[1]


def pack_kernel(spans, other, *refs):
    blocks, outs = refs[: -len(spans)], refs[-len(spans) :]
    for (start, stop), out in zip(spans, outs):
        for n, block in enumerate(blocks):
            out[2 * n] = block[0, :, start:stop]
            out[2 * n + 1] = other[n, :, start:stop]


def order_kernel(*refs):
    hiddens, right = refs[:-1], refs[-1]
    ways, flight = right.shape[:2]
    _, lane, own = seat_of(ways)
    for dj, hidden in enumerate(hiddens):
        for n, d in enumerate(turns(ways)):
            for dg in range(flight):
                right[n, dg, dj] = hidden[lane ^ d, own ^ dg]


def update_kernel(start, stop, *refs):
    refs = list(refs)
    rows = refs[:-9]
    right, master, first, second, fresh, new_master, new_first, new_second, gradient = refs[-9:]
    hidden = right[...].reshape(-1, right.shape[-1])
    left = tall([block[...].reshape(-1, stop - start) for block in rows])
    gradient[...] = lax.dot_general(
        left, hidden, (((0,), (0,)), ((), ())), preferred_element_type=f32
    )
    for low in range(start, stop, 128):
        end = min(low + 128, stop)
        here = pl.ds(low, end - low)
        there = pl.ds(low - start, end - low)
        grad = gradient[there]
        old = master[here]
        moment_a = beta_one * first[here] + (1.0 - beta_one) * grad
        moment_b = beta_two * second[here] + (1.0 - beta_two) * grad * grad
        step_size = (moment_a * (1.0 / (1.0 - beta_one**5))) / (
            jnp.sqrt(moment_b * (1.0 / (1.0 - beta_two**5))) + epsilon
        )
        updated = old - learning_rate * (step_size + decay_rate * old)
        fresh[there] = updated.astype(bf16)
        new_master[there] = updated
        new_first[there] = moment_a
        new_second[there] = moment_b


def partial_kernel(spans, kept, *refs):
    refs = list(refs)
    chunks = len(spans)
    keep, send, own_fresh, held = refs[-4:]
    ways = held.shape[0]
    rows, fresh, (master,) = take(refs, ways * chunks), take(refs, chunks), take(refs, 1)
    flight = held.shape[1]
    _, lane, own = seat_of(ways)
    left = wide(
        [
            tall([block[...].reshape(-1, stop - start) for block in rows[c * ways : (c + 1) * ways]])
            for c, (start, stop) in enumerate(spans)
        ]
    )
    share = jnp.dot(left, master[...].astype(bf16), preferred_element_type=f32)
    held[...] = share.reshape(held.shape)
    for out, chosen in ((keep, kept[0]), (send, kept[1])):
        for n, dj in enumerate(chosen):
            for at, d in enumerate(turns(ways)):
                for dg in range(flight):
                    out[n, lane ^ d, own ^ dg] = held[at, dg, dj].astype(out.dtype)
    for c, (start, stop) in enumerate(spans):
        own_fresh[start:stop] = fresh[c][...]


def halve_kernel(kept, held, arrived, keep, send):
    for out, chosen in ((keep, kept[0]), (send, kept[1])):
        for n, m in enumerate(chosen):
            out[n] = (held[m] + arrived[m].astype(f32)).astype(out.dtype)


def store_kernel(spans, *refs):
    refs = list(refs)
    news = take(refs, 3 * len(spans))
    outs = take(refs, 3)
    (sems,) = refs
    copies = []
    for c, (start, stop) in enumerate(spans):
        for n in range(3):
            copy = pltpu.make_async_copy(
                news[3 * c + n], outs[n].at[pl.ds(start, stop - start)], sems.at[c, n]
            )
            copy.start()
            copies.append(copy)
    for copy in copies:
        copy.wait()


def gate_kernel(gate, up, held, arrived, d_gate, d_up):
    ways, flight, slots = held.shape[1:4]
    for f in range(flight):
        for v in range(ways):
            at = pl.ds((f * ways + v) * slots, slots)
            grad = held[0, v, f] + arrived[0, v, f].astype(f32)
            g = gate[0, at].astype(f32)
            u = up[0, at].astype(f32)
            sig = jax.nn.sigmoid(g)
            d_gate[0, at] = (grad * u * sig * (1.0 + g * (1.0 - sig))).astype(bf16)
            d_up[0, at] = (grad * (g * sig)).astype(bf16)


def join_kernel(high, entries, *refs):
    out, sems = refs[-2], refs[-1]
    me = lax.axis_index("dp")
    copies = []
    for n, (d, start, stop) in enumerate(entries):
        at = pl.multiple_of((me ^ d) * high + start, 16)
        copy = pltpu.make_async_copy(refs[n], out.at[pl.ds(at, stop - start)], sems.at[n])
        copy.start()
        copies.append(copy)
    for copy in copies:
        copy.wait()


def whole(memory=pltpu.VMEM):
    return pl.BlockSpec(memory_space=memory)


def shape(dims, kind):
    return jax.ShapeDtypeStruct(dims, kind)


def pinned(x):
    return pltpu.with_memory_space_constraint(x, pltpu.HBM)


def local(
    grad_rows,
    router_weight,
    send_counts,
    gate_stash,
    up_stash,
    master_weight,
    first_moment,
    second_moment,
):
    _, flight, slots, width = grad_rows.shape
    pieces = lax.axis_size("dp")
    sources = lax.axis_size("expert")
    ways = sources // flight
    high, across = master_weight.shape
    hbm = whole(pltpu.HBM)
    count = pieces * flight * slots

    def over_dp(x, d):
        return lax.ppermute(x, "dp", [(i, i ^ d) for i in range(pieces)])

    tiles = -(-high // LANES)
    middle = (tiles + 1) // 2 * LANES
    spans = [(0, middle), (middle, high)] if middle < high else [(0, high)]
    offsets = [(dj, dg) for dg in range(flight) for dj in range(0, pieces, 2)]
    results = pl.pallas_call(
        scale_kernel,
        out_shape=[shape((ways, flight, slots, across), bf16)]
        + [shape((2, slots, high), bf16)] * len(offsets),
        in_specs=[hbm] * 5,
        out_specs=[whole()] * (1 + len(offsets)),
        scratch_shapes=[
            pltpu.SMEM(send_counts.shape, jnp.int32),
            pltpu.VMEM(router_weight.shape, f32),
            pltpu.VMEM(grad_rows.shape, bf16),
            pltpu.VMEM(gate_stash.shape, bf16),
            pltpu.VMEM(up_stash.shape, bf16),
            pltpu.VMEM((pieces, flight, slots, high), bf16),
            pltpu.SemaphoreType.DMA((5,)),
        ],
        compiler_params=params(),
        name="scale",
    )(
        pinned(send_counts),
        pinned(router_weight),
        pinned(grad_rows),
        pinned(gate_stash),
        pinned(up_stash),
    )
    hidden, blocks = results[0], list(results[1:])
    for n, (dj, dg) in reversed(list(enumerate(offsets))):
        if n:
            pairs = [
                (i * sources + k, (i ^ dj) * sources + (k ^ (dg * ways)))
                for i in range(pieces)
                for k in range(sources)
            ]
            blocks[n] = lax.ppermute(blocks[n], ("dp", "expert"), pairs)
    state = pl.pallas_call(
        fetch_kernel,
        out_shape=[shape((high, across), f32)] * 3,
        in_specs=[whole(pl.ANY)] + [hbm] * 3,
        out_specs=[whole()] * 3,
        scratch_shapes=[pltpu.SemaphoreType.DMA((3,))],
        compiler_params=params(),
        cost_estimate=cost(0, high * across * 24),
        name="fetch",
    )(hidden, pinned(master_weight), pinned(first_moment), pinned(second_moment))
    order = [*range(pieces // 2, len(offsets)), *range(1, pieces // 2), 0]
    turned, state = lax.optimization_barrier(([blocks[n] for n in order], state))
    blocks = [turned[order.index(n)] for n in range(len(offsets))]
    other = pl.pallas_call(
        functools.partial(share_kernel, order),
        out_shape=shape((len(offsets), slots, high), bf16),
        in_specs=[whole()] * len(offsets),
        out_specs=whole(),
        compiler_params=params(),
        name="share",
    )(*[blocks[n] for n in order])
    mine = pl.pallas_call(
        functools.partial(pack_kernel, spans),
        out_shape=[shape((2 * len(offsets), slots, stop - start), bf16) for start, stop in spans],
        in_specs=[whole()] * (1 + len(offsets)),
        out_specs=[whole()] * len(spans),
        compiler_params=params(),
        name="pack",
    )(over_dp(other, 1), *blocks)
    top = pieces // 2

    def spread(entries, first):
        step = first
        while step:
            entries = entries + [(d ^ step, *span, over_dp(x, step)) for d, *span, x in entries]
            step //= 2
        return entries

    hiddens = [entry[1] for entry in sorted(spread([(0, hidden)], top), key=lambda e: e[0])]
    right = pl.pallas_call(
        order_kernel,
        out_shape=shape((ways, flight, pieces, slots, across), bf16),
        in_specs=[whole()] * pieces,
        out_specs=whole(),
        compiler_params=params(),
        name="order",
    )(*hiddens)
    rows = []
    for piece in mine:
        rows.append(
            [piece]
            + [
                lax.ppermute(piece, "expert", [(k, k ^ d) for k in range(sources)])
                for d in turns(ways)[1:]
            ]
        )

    fresh, news = [], []
    for c, (start, stop) in enumerate(spans):
        out = pl.pallas_call(
            functools.partial(update_kernel, start, stop),
            out_shape=[shape((stop - start, across), bf16)]
            + [shape((stop - start, across), f32)] * 3,
            in_specs=[whole()] * (ways + 4),
            out_specs=[whole()] * 4,
            scratch_shapes=[pltpu.VMEM((stop - start, across), f32)],
            compiler_params=params(),
            cost_estimate=cost(2 * ways * count * (stop - start) * across, high * across * 26),
            name="update",
        )(*rows[c], right, *state)
        fresh.append(out[0])
        news += out[1:]
    crossed = [over_dp(piece, top) for piece in fresh]

    part = (ways, flight, slots, across)
    bit = 1
    kept = [[d for d in range(pieces) if not d & bit], [d for d in range(pieces) if d & bit]]
    keep, send, own_fresh = pl.pallas_call(
        functools.partial(partial_kernel, spans, kept),
        out_shape=[
            shape((pieces // 2, *part), f32),
            shape((pieces // 2, *part), bf16),
            shape((high, across), bf16),
        ],
        in_specs=[whole()] * ((ways + 1) * len(spans) + 1),
        out_specs=[whole()] * 3,
        scratch_shapes=[pltpu.VMEM((ways, flight, pieces, slots, across), f32)],
        compiler_params=params(),
        cost_estimate=cost(2 * ways * count * high * across, high * across * 12),
        name="partial",
    )(*[block for chunk in rows for block in chunk], *fresh, state[0])
    arrived = over_dp(send, bit)
    while bit < top:
        bit *= 2
        left = kept[0]
        kept = [[d for d in left if not d & bit], [d for d in left if d & bit]]
        chosen = [[left.index(d) for d in half] for half in kept]
        keep, send = pl.pallas_call(
            functools.partial(halve_kernel, chosen),
            out_shape=[
                shape((len(kept[0]), *part), f32),
                shape((len(kept[1]), *part), bf16),
            ],
            in_specs=[whole()] * 2,
            out_specs=[whole()] * 2,
            compiler_params=params(),
            name="halve",
        )(keep, arrived)
        arrived = over_dp(send, bit)
    if len(spans) > 1:
        crossed[0], keep = lax.optimization_barrier((crossed[0], keep))
    d_gate, d_up = pl.pallas_call(
        gate_kernel,
        out_shape=[shape(gate_stash.shape, bf16)] * 2,
        in_specs=[whole()] * 4,
        out_specs=[whole()] * 2,
        compiler_params=params(),
        name="gates",
    )(gate_stash, up_stash, keep, arrived)

    states = pl.pallas_call(
        functools.partial(store_kernel, spans),
        out_shape=[shape((high, across), f32)] * 3,
        in_specs=[whole()] * len(news),
        out_specs=[hbm] * 3,
        scratch_shapes=[pltpu.SemaphoreType.DMA((len(spans), 3))],
        compiler_params=params(),
        cost_estimate=cost(0, high * across * 24),
        name="store",
    )(*news)

    def join(entries, before):
        return pl.pallas_call(
            functools.partial(join_kernel, high, [entry[:3] for entry in entries]),
            out_shape=shape((pieces * high, across), bf16),
            in_specs=[whole(pl.ANY)] * len(entries) + [hbm] * len(before),
            out_specs=hbm,
            input_output_aliases={len(entries): 0} if before else {},
            scratch_shapes=[pltpu.SemaphoreType.DMA((len(entries),))],
            compiler_params=params(),
            name="join",
        )(*[entry[3] for entry in entries], *before)

    near, *far = spread([(0, 0, high, own_fresh)], top // 2)
    early, late = [near], far
    for (start, stop), piece in zip(spans[:-1], crossed[:-1]):
        near, *far = spread([(top, start, stop, piece)], top // 2)
        early.append(near)
        late += far
    joined = join(early, [])
    crossed[-1], joined, states, arrived = lax.optimization_barrier(
        (crossed[-1], joined, states, arrived)
    )
    joined = join(late + spread([(top, *spans[-1], crossed[-1])], top // 2), [joined])
    return (d_gate, d_up, *states, joined)


def solution(mesh):
    placed = (
        P("dp", "expert", None, None),
        P("dp", "expert", None),
        P("dp", "expert"),
        P("dp", None, "expert"),
        P("dp", None, "expert"),
        P("dp", "expert"),
        P("dp", "expert"),
        P("dp", "expert"),
    )
    return jax.shard_map(
        local,
        mesh=mesh,
        in_specs=placed,
        out_specs=(
            P("dp", None, "expert"),
            P("dp", None, "expert"),
            P("dp", "expert"),
            P("dp", "expert"),
            P("dp", "expert"),
            P(None, "expert"),
        ),
        check_vma=False,
    )
```

profile of v0, /device:TPU:0, one launch (start us, length us, event | category | flops | bytes accessed | tf_op | source)
XLA Modules:
  0.0 40.1 jit_solution(13274683435050901986)
XLA Ops:
  0.6 1.2 %scale.1 = (bf16[4,2,16,256]{3,2,1,0:T(8,128)(2,1)S(1)}, bf16[2,16,896]{2,1,0:T(8,128)(2,1)S(1)}, bf16[2,16,896]{2,1,0:T(8,128)(2,1)S(1)}, bf16[2,16,896]{2,1,0:T(8,128)(2,1)S(1)}, bf16[2,16,896]{2,1,0:T(8,128)(2,1)S(1)}) custom-call(s32[1,2]{1,0:T(1,128)} %counts_in.1, f32[1,2,16]{2,1,0:T(2,128)} %router_in.1, bf16[1,2,16,3584]{3,2,1,0:T(8,128)(2,1)} %rows_in.1, ...), custom_call_target="tpu_custom_call" | custom-call | tf_op jit(solution)/shard_map/scale/pallas_call | solution.py:275
  1.9 4.1 %collective-permute-start = (bf16[2,16,896]{2,1,0:T(8,128)(2,1)S(1)}, bf16[2,16,896]{2,1,0:T(8,128)(2,1)S(1)}, u32[]{:S(2)}, u32[]{:S(2)}) collective-permute-start(bf16[2,16,896]{2,1,0:T(8,128)(2,1)S(1)} %get-tuple-element.48), channel_id=1, source_target_pairs={{0,4},{1,5},{2,6},{3,7},{4,0},{5,1},{6,2},{7,3},{8,12},{9,13},{10,... | collective-permute-start | bytes 172040 | tf_op jit(solution)/shard_map/ppermute | solution.py:307
  6.0 1.3 %collective-permute-start.1 = (bf16[2,16,896]{2,1,0:T(8,128)(2,1)S(1)}, bf16[2,16,896]{2,1,0:T(8,128)(2,1)S(1)}, u32[]{:S(2)}, u32[]{:S(2)}) collective-permute-start(bf16[2,16,896]{2,1,0:T(8,128)(2,1)S(1)} %get-tuple-element.49), channel_id=1, source_target_pairs={{0,20},{1,21},{2,22},{3,23},{4,16},{5,17},{6,18},{7,19},{8,28},{9,... | collective-permute-start | bytes 172040 | tf_op jit(solution)/shard_map/ppermute | solution.py:307
  7.2 0.3 collective-permute-start.2
  7.5 1.8 %fetch.1 = (f32[896,256]{1,0:T(8,128)S(1)}, f32[896,256]{1,0:T(8,128)S(1)}, f32[896,256]{1,0:T(8,128)S(1)}) custom-call(bf16[4,2,16,256]{3,2,1,0:T(8,128)(2,1)S(1)} %get-tuple-element.52.after.refs_0_, f32[896,256]{1,0:T(8,128)} %refs_0_.1, f32[896,256]{1,0:T(8,128)} %refs_1_.1, f32[896,256]{1,0:T(8,128)} %refs_2_.1), custom_call_target="tpu_custom_call" | custom-call | bytes 5505024 | tf_op jit(solution)/shard_map/fetch/pallas_call | solution.py:308
  9.3 0.0 collective-permute-done.refs_0_.refs_2_
  9.3 3.0 %collective-permute-done.1.refs_1_.refs_3_ = bf16[2,16,896]{2,1,0:T(8,128)(2,1)S(1)} collective-permute-done((bf16[2,16,896]{2,1,0:T(8,128)(2,1)S(1)}, bf16[2,16,896]{2,1,0:T(8,128)(2,1)S(1)}, u32[]{:S(2)}, u32[]{:S(2)}) %collective-permute-start.1) | collective-permute-done | bytes 57376 | tf_op jit(solution)/shard_map/ppermute | solution.py:307
  12.3 0.0 collective-permute-done.2.refs_2_.refs_1_
  12.3 0.1 collective-permute-start.3
  12.4 1.4 %collective-permute-start.8 = (bf16[4,2,16,256]{3,2,1,0:T(8,128)(2,1)S(1)}, bf16[4,2,16,256]{3,2,1,0:T(8,128)(2,1)S(1)}, u32[]{:S(2)}, u32[]{:S(2)}) collective-permute-start(bf16[4,2,16,256]{3,2,1,0:T(8,128)(2,1)S(1)} %get-tuple-element.52.after.refs_0_), channel_id=1, source_target_pairs={{0,16},{8,24},{16,0},{24,8},{1,17},{9,25},{17,1},{25,9},{2,18},{10... | collective-permute-start | bytes 196616 | tf_op jit(solution)/shard_map/ppermute | solution.py:269
  13.8 0.0 collective-permute-done.3.other
  13.8 1.6 %collective-permute-start.6 = (bf16[8,16,512]{2,1,0:T(8,128)(2,1)S(1)}, bf16[8,16,512]{2,1,0:T(8,128)(2,1)S(1)}, u32[]{:S(2)}, u32[]{:S(2)}) collective-permute-start(bf16[8,16,512]{2,1,0:T(8,128)(2,1)S(1)} %get-tuple-element.60.refs_0_), channel_id=1, source_target_pairs={{0,1},{1,0},{2,3},{3,2},{4,5},{5,4},{6,7},{7,6},{8,9},{9,8},{10,11... | collective-permute-start | bytes 393224 | tf_op jit(solution)/shard_map/ppermute | solution.py:360
  15.4 1.4 %collective-permute-start.5 = (bf16[8,16,512]{2,1,0:T(8,128)(2,1)S(1)}, bf16[8,16,512]{2,1,0:T(8,128)(2,1)S(1)}, u32[]{:S(2)}, u32[]{:S(2)}) collective-permute-start(bf16[8,16,512]{2,1,0:T(8,128)(2,1)S(1)} %get-tuple-element.60.refs_0_), channel_id=1, source_target_pairs={{0,2},{1,3},{2,0},{3,1},{4,6},{5,7},{6,4},{7,5},{8,10},{9,11},{10,... | collective-permute-start | bytes 393224 | tf_op jit(solution)/shard_map/ppermute | solution.py:360
  16.8 0.6 %collective-permute-start.4 = (bf16[8,16,512]{2,1,0:T(8,128)(2,1)S(1)}, bf16[8,16,512]{2,1,0:T(8,128)(2,1)S(1)}, u32[]{:S(2)}, u32[]{:S(2)}) collective-permute-start(bf16[8,16,512]{2,1,0:T(8,128)(2,1)S(1)} %get-tuple-element.60.refs_0_), channel_id=1, source_target_pairs={{0,3},{1,2},{2,1},{3,0},{4,7},{5,6},{6,5},{7,4},{8,11},{9,10},{10,... | collective-permute-start | bytes 393224 | tf_op jit(solution)/shard_map/ppermute | solution.py:360
  17.4 0.0 collective-permute-start.7
  17.4 0.0 collective-permute-done.8.refs_2_
  17.4 0.5 %collective-permute-start.9 = (bf16[4,2,16,256]{3,2,1,0:T(8,128)(2,1)S(1)}, bf16[4,2,16,256]{3,2,1,0:T(8,128)(2,1)S(1)}, u32[]{:S(2)}, u32[]{:S(2)}) collective-permute-start(bf16[4,2,16,256]{3,2,1,0:T(8,128)(2,1)S(1)} %collective-permute-done.8.refs_2_), channel_id=1, source_target_pairs={{0,8},{8,0},{16,24},{24,16},{1,9},{9,1},{17,25},{25,17},{2,10},{10... | collective-permute-start | bytes 196616 | tf_op jit(solution)/shard_map/ppermute | solution.py:269
  17.9 0.7 %collective-permute-done.7.refs_1_ = bf16[4,2,16,256]{3,2,1,0:T(8,128)(2,1)S(1)} collective-permute-done((bf16[4,2,16,256]{3,2,1,0:T(8,128)(2,1)S(1)}, bf16[4,2,16,256]{3,2,1,0:T(8,128)(2,1)S(1)}, u32[]{:S(2)}, u32[]{:S(2)}) %collective-permute-start.7) | collective-permute-done | bytes 65568 | tf_op jit(solution)/shard_map/ppermute | solution.py:269
  18.6 1.5 %collective-permute-start.13 = (bf16[8,16,384]{2,1,0:T(8,128)(2,1)S(1)}, bf16[8,16,384]{2,1,0:T(8,128)(2,1)S(1)}, u32[]{:S(2)}, u32[]{:S(2)}) collective-permute-start(bf16[8,16,384]{2,1,0:T(8,128)(2,1)S(1)} %get-tuple-element.65.refs_0_.refs_4_), channel_id=1, source_target_pairs={{0,1},{1,0},{2,3},{3,2},{4,5},{5,4},{6,7},{7,6},{8,9},{9,8},{10,11... | collective-permute-start | bytes 294920 | tf_op jit(solution)/shard_map/ppermute | solution.py:360
  20.2 0.0 collective-permute-done.9.refs_3_
  20.2 1.4 %collective-permute-start.12 = (bf16[8,16,384]{2,1,0:T(8,128)(2,1)S(1)}, bf16[8,16,384]{2,1,0:T(8,128)(2,1)S(1)}, u32[]{:S(2)}, u32[]{:S(2)}) collective-permute-start(bf16[8,16,384]{2,1,0:T(8,128)(2,1)S(1)} %get-tuple-element.65.refs_0_.refs_4_), channel_id=1, source_target_pairs={{0,2},{1,3},{2,0},{3,1},{4,6},{5,7},{6,4},{7,5},{8,10},{9,11},{10,... | collective-permute-start | bytes 294920 | tf_op jit(solution)/shard_map/ppermute | solution.py:360
  21.5 0.0 collective-permute-done.6.refs_3_
  21.5 0.6 %collective-permute-start.11 = (bf16[8,16,384]{2,1,0:T(8,128)(2,1)S(1)}, bf16[8,16,384]{2,1,0:T(8,128)(2,1)S(1)}, u32[]{:S(2)}, u32[]{:S(2)}) collective-permute-start(bf16[8,16,384]{2,1,0:T(8,128)(2,1)S(1)} %get-tuple-element.65.refs_0_.refs_4_), channel_id=1, source_target_pairs={{0,3},{1,2},{2,1},{3,0},{4,7},{5,6},{6,5},{7,4},{8,11},{9,10},{10,... | collective-permute-start | bytes 294920 | tf_op jit(solution)/shard_map/ppermute | solution.py:360
  22.2 0.0 collective-permute-done.5.refs_2_
  22.2 2.1 %collective-permute-done.4.refs_1_ = bf16[8,16,512]{2,1,0:T(8,128)(2,1)S(1)} collective-permute-done((bf16[8,16,512]{2,1,0:T(8,128)(2,1)S(1)}, bf16[8,16,512]{2,1,0:T(8,128)(2,1)S(1)}, u32[]{:S(2)}, u32[]{:S(2)}) %collective-permute-start.4) | collective-permute-done | bytes 131104 | tf_op jit(solution)/shard_map/ppermute | solution.py:360
  24.3 0.7 %update.2 = (bf16[512,256]{1,0:T(8,128)(2,1)S(1)}, f32[512,256]{1,0:T(8,128)S(1)}, f32[512,256]{1,0:T(8,128)S(1)}, f32[512,256]{1,0:T(8,128)S(1)}) custom-call(bf16[8,16,512]{2,1,0:T(8,128)(2,1)S(1)} %get-tuple-element.60.refs_0_, bf16[8,16,512]{2,1,0:T(8,128)(2,1)S(1)} %collective-permute-done.4.refs_1_, ...), custom_call_target="tpu_custom_call" | custom-call | flops 134217728 | bytes 5963776 | tf_op jit(solution)/shard_map/update/pallas_call | solution.py:367
  25.0 1.2 %collective-permute-start.10 = (bf16[512,256]{1,0:T(8,128)(2,1)S(1)}, bf16[512,256]{1,0:T(8,128)(2,1)S(1)}, u32[]{:S(2)}, u32[]{:S(2)}) collective-permute-start(bf16[512,256]{1,0:T(8,128)(2,1)S(1)} %get-tuple-element.64.refs_8_), channel_id=1, source_target_pairs={{0,16},{8,24},{16,0},{24,8},{1,17},{9,25},{17,1},{25,9},{2,18},{10... | collective-permute-start | bytes 786440 | tf_op jit(solution)/shard_map/ppermute | solution.py:269
  26.2 0.1 collective-permute-done.13.refs_3_.refs_7_
  26.3 0.2 collective-permute-done.12.refs_2_.refs_6_
  26.4 1.3 %collective-permute-done.11.refs_1_.refs_5_ = bf16[8,16,384]{2,1,0:T(8,128)(2,1)S(1)} collective-permute-done((bf16[8,16,384]{2,1,0:T(8,128)(2,1)S(1)}, bf16[8,16,384]{2,1,0:T(8,128)(2,1)S(1)}, u32[]{:S(2)}, u32[]{:S(2)}) %collective-permute-start.11) | collective-permute-done | bytes 98336 | tf_op jit(solution)/shard_map/ppermute | solution.py:360
  27.7 0.6 %update.3 = (bf16[384,256]{1,0:T(8,128)(2,1)S(1)}, f32[384,256]{1,0:T(8,128)S(1)}, f32[384,256]{1,0:T(8,128)S(1)}, f32[384,256]{1,0:T(8,128)S(1)}) custom-call(bf16[8,16,384]{2,1,0:T(8,128)(2,1)S(1)} %get-tuple-element.65.refs_0_.refs_4_, bf16[8,16,384]{2,1,0:T(8,128)(2,1)S(1)} %collective-permute-done.11.refs_1_.refs_5_, ...), custom_call_target="tpu_custom_call" | custom-call | flops 100663296 | bytes 5963776 | tf_op jit(solution)/shard_map/update/pallas_call | solution.py:367
  28.3 0.4 %partial.1 = (f32[2,4,2,16,256]{4,3,2,1,0:T(8,128)S(1)}, bf16[2,4,2,16,256]{4,3,2,1,0:T(8,128)(2,1)S(1)}, bf16[896,256]{1,0:T(8,128)(2,1)S(1)}) custom-call(bf16[8,16,512]{2,1,0:T(8,128)(2,1)S(1)} %get-tuple-element.60.refs_0_, bf16[8,16,512]{2,1,0:T(8,128)(2,1)S(1)} %collective-permute-done.4.refs_1_, ...), custom_call_target="tpu_custom_call" | custom-call | flops 234881024 | bytes 2752512 | tf_op jit(solution)/shard_map/partial/pallas_call | solution.py:385
  28.7 0.1 collective-permute-start.17
  28.8 0.5 %collective-permute-start.14 = (bf16[2,4,2,16,256]{4,3,2,1,0:T(8,128)(2,1)S(1)}, bf16[2,4,2,16,256]{4,3,2,1,0:T(8,128)(2,1)S(1)}, u32[]{:S(2)}, u32[]{:S(2)}) collective-permute-start(bf16[2,4,2,16,256]{4,3,2,1,0:T(8,128)(2,1)S(1)} %get-tuple-element.68), channel_id=1, source_target_pairs={{0,8},{8,0},{16,24},{24,16},{1,9},{9,1},{17,25},{25,17},{2,10},{10... | collective-permute-start | bytes 393224 | tf_op jit(solution)/shard_map/ppermute | solution.py:269
  29.3 1.2 %collective-permute-start.16 = (bf16[384,256]{1,0:T(8,128)(2,1)S(1)}, bf16[384,256]{1,0:T(8,128)(2,1)S(1)}, u32[]{:S(2)}, u32[]{:S(2)}) collective-permute-start(bf16[384,256]{1,0:T(8,128)(2,1)S(1)} %get-tuple-element.66.refs_9_), channel_id=1, source_target_pairs={{0,16},{8,24},{16,0},{24,8},{1,17},{9,25},{17,1},{25,9},{2,18},{10... | collective-permute-start | bytes 589832 | tf_op jit(solution)/shard_map/ppermute | solution.py:269
  30.5 0.3 collective-permute-done.14.arrived
  30.8 1.3 %collective-permute-start.15 = (bf16[1,4,2,16,256]{4,3,2,1,0:T(8,128)(2,1)S(1)}, bf16[1,4,2,16,256]{4,3,2,1,0:T(8,128)(2,1)S(1)}, u32[]{:S(2)}, u32[]{:S(2)}) collective-permute-start(bf16[1,4,2,16,256]{4,3,2,1,0:T(8,128)(2,1)S(1)} %get-tuple-element.71), channel_id=1, source_target_pairs={{0,16},{8,24},{16,0},{24,8},{1,17},{9,25},{17,1},{25,9},{2,18},{10... | collective-permute-start | bytes 196616 | tf_op jit(solution)/shard_map/ppermute | solution.py:269
  32.1 0.0 collective-permute-done.10.refs_1_
  32.1 0.0 collective-permute-start.18
  32.1 1.6 %store.1 = (f32[896,256]{1,0:T(8,128)}, f32[896,256]{1,0:T(8,128)}, f32[896,256]{1,0:T(8,128)}) custom-call(f32[512,256]{1,0:T(8,128)S(1)} %get-tuple-element.76.refs_0_, f32[512,256]{1,0:T(8,128)S(1)} %get-tuple-element.77.refs_1_, f32[512,256]{1,0:T(8,128)S(1)} %get-tuple-element.78.refs_2_, f32[384,256]{1,0:T(8,128)S(1)} %get-tuple-element.79.refs_3_, ...), custom_call_target="tpu_custom_call" | custom-call | bytes 5505024 | tf_op jit(solution)/shard_map/store/pallas_call | solution.py:428
  33.7 0.0 copy-start
  33.7 0.0 copy-start.1
  33.7 0.9 %join.2.refs_4_ = bf16[3584,256]{1,0:T(8,128)(2,1)} custom-call(bf16[896,256]{1,0:T(8,128)(2,1)S(1)} %get-tuple-element.74.refs_0_, bf16[512,256]{1,0:T(8,128)(2,1)S(1)} %collective-permute-done.10.refs_1_), custom_call_target="tpu_custom_call" | custom-call | tf_op jit(solution)/shard_map/join/pallas_call | solution.py:440
  34.6 2.3 %collective-permute-done.16.refs_2_ = bf16[384,256]{1,0:T(8,128)(2,1)S(1)} collective-permute-done((bf16[384,256]{1,0:T(8,128)(2,1)S(1)}, bf16[384,256]{1,0:T(8,128)(2,1)S(1)}, u32[]{:S(2)}, u32[]{:S(2)}) %collective-permute-start.16) | collective-permute-done | bytes 196640 | tf_op jit(solution)/shard_map/ppermute | solution.py:269
  36.9 0.7 %collective-permute-done.15.arrived = bf16[1,4,2,16,256]{4,3,2,1,0:T(8,128)(2,1)S(1)} collective-permute-done((bf16[1,4,2,16,256]{4,3,2,1,0:T(8,128)(2,1)S(1)}, bf16[1,4,2,16,256]{4,3,2,1,0:T(8,128)(2,1)S(1)}, u32[]{:S(2)}, u32[]{:S(2)}) %collective-permute-start.15) | collective-permute-done | bytes 65568 | tf_op jit(solution)/shard_map/ppermute | solution.py:269
  37.6 0.0 collective-permute-start.19
  37.6 0.0 copy-done
  37.6 0.0 copy-done.1
  37.6 0.7 %gates.1 = (bf16[1,128,256]{2,1,0:T(8,128)(2,1)}, bf16[1,128,256]{2,1,0:T(8,128)(2,1)}) custom-call(bf16[1,128,256]{2,1,0:T(8,128)(2,1)S(1)} %copy-done, bf16[1,128,256]{2,1,0:T(8,128)(2,1)S(1)} %copy-done.1, f32[1,4,2,16,256]{4,3,2,1,0:T(8,128)S(1)} %get-tuple-element.70.held, bf16[1,4,2,16,256]{4,3,2,1,0:T(8,128)(2,1)S(1)} %collective-permute-done.15.arrived), custom_call_target="tpu_custom_call" | custom-call | tf_op jit(solution)/shard_map/gates/pallas_call | solution.py:419
  38.3 0.7 %collective-permute-done.19.refs_3_ = bf16[384,256]{1,0:T(8,128)(2,1)S(1)} collective-permute-done((bf16[384,256]{1,0:T(8,128)(2,1)S(1)}, bf16[384,256]{1,0:T(8,128)(2,1)S(1)}, u32[]{:S(2)}, u32[]{:S(2)}) %collective-permute-start.19) | collective-permute-done | bytes 196640 | tf_op jit(solution)/shard_map/ppermute | solution.py:269
  39.0 0.0 collective-permute-done.17.refs_0_
  39.0 0.0 collective-permute-done.18.refs_1_
  39.0 1.0 %join.3 = bf16[3584,256]{1,0:T(8,128)(2,1)} custom-call(bf16[896,256]{1,0:T(8,128)(2,1)S(1)} %collective-permute-done.17.refs_0_, bf16[512,256]{1,0:T(8,128)(2,1)S(1)} %collective-permute-done.18.refs_1_, bf16[384,256]{1,0:T(8,128)(2,1)S(1)} %collective-permute-done.16.refs_2_, ...), custom_call_target="tpu_custom_call", output_to_operand_aliasing={{}: (4, {})} | custom-call | tf_op jit(solution)/shard_map/join/pallas_call | solution.py:440
  (4 shorter events, 0.1 us)
Async XLA Ops:
  1.9 7.4 %collective-permute-start = (bf16[2,16,896]{2,1,0:T(8,128)(2,1)S(1)}, bf16[2,16,896]{2,1,0:T(8,128)(2,1)S(1)}, u32[]{:S(2)}, u32[]{:S(2)}) collective-permute-start(bf16[2,16,896]{2,1,0:T(8,128)(2,1)S(1)} %get-tuple-element.48), channel_id=1, source_target_pairs={{0,4},{1,5},{2,6},{3,7},{4,0},{5,1},{6,2},{7,3},{8,12},{9,13},{10,... | collective-permute-start | bytes 172040 | tf_op jit(solution)/shard_map/ppermute | solution.py:307
  6.0 6.4 %collective-permute-start.1 = (bf16[2,16,896]{2,1,0:T(8,128)(2,1)S(1)}, bf16[2,16,896]{2,1,0:T(8,128)(2,1)S(1)}, u32[]{:S(2)}, u32[]{:S(2)}) collective-permute-start(bf16[2,16,896]{2,1,0:T(8,128)(2,1)S(1)} %get-tuple-element.49), channel_id=1, source_target_pairs={{0,20},{1,21},{2,22},{3,23},{4,16},{5,17},{6,18},{7,19},{8,28},{9,... | collective-permute-start | bytes 172040 | tf_op jit(solution)/shard_map/ppermute | solution.py:307
  7.2 5.1 %collective-permute-start.2 = (bf16[2,16,896]{2,1,0:T(8,128)(2,1)S(1)}, bf16[2,16,896]{2,1,0:T(8,128)(2,1)S(1)}, u32[]{:S(2)}, u32[]{:S(2)}) collective-permute-start(bf16[2,16,896]{2,1,0:T(8,128)(2,1)S(1)} %get-tuple-element.50), channel_id=1, source_target_pairs={{0,16},{1,17},{2,18},{3,19},{4,20},{5,21},{6,22},{7,23},{8,24},{9,... | collective-permute-start | bytes 172040 | tf_op jit(solution)/shard_map/ppermute | solution.py:307
  12.3 1.5 %collective-permute-start.3 = (bf16[4,16,896]{2,1,0:T(8,128)(2,1)S(1)}, bf16[4,16,896]{2,1,0:T(8,128)(2,1)S(1)}, u32[]{:S(2)}, u32[]{:S(2)}) collective-permute-start(bf16[4,16,896]{2,1,0:T(8,128)(2,1)S(1)} %share.1), channel_id=1, source_target_pairs={{0,8},{8,0},{16,24},{24,16},{1,9},{9,1},{17,25},{25,17},{2,10},{10... | collective-permute-start | bytes 344072 | tf_op jit(solution)/shard_map/ppermute | solution.py:269
  12.4 5.0 %collective-permute-start.8 = (bf16[4,2,16,256]{3,2,1,0:T(8,128)(2,1)S(1)}, bf16[4,2,16,256]{3,2,1,0:T(8,128)(2,1)S(1)}, u32[]{:S(2)}, u32[]{:S(2)}) collective-permute-start(bf16[4,2,16,256]{3,2,1,0:T(8,128)(2,1)S(1)} %get-tuple-element.52.after.refs_0_), channel_id=1, source_target_pairs={{0,16},{8,24},{16,0},{24,8},{1,17},{9,25},{17,1},{25,9},{2,18},{10... | collective-permute-start | bytes 196616 | tf_op jit(solution)/shard_map/ppermute | solution.py:269
  13.8 7.7 %collective-permute-start.6 = (bf16[8,16,512]{2,1,0:T(8,128)(2,1)S(1)}, bf16[8,16,512]{2,1,0:T(8,128)(2,1)S(1)}, u32[]{:S(2)}, u32[]{:S(2)}) collective-permute-start(bf16[8,16,512]{2,1,0:T(8,128)(2,1)S(1)} %get-tuple-element.60.refs_0_), channel_id=1, source_target_pairs={{0,1},{1,0},{2,3},{3,2},{4,5},{5,4},{6,7},{7,6},{8,9},{9,8},{10,11... | collective-permute-start | bytes 393224 | tf_op jit(solution)/shard_map/ppermute | solution.py:360
  15.4 6.7 %collective-permute-start.5 = (bf16[8,16,512]{2,1,0:T(8,128)(2,1)S(1)}, bf16[8,16,512]{2,1,0:T(8,128)(2,1)S(1)}, u32[]{:S(2)}, u32[]{:S(2)}) collective-permute-start(bf16[8,16,512]{2,1,0:T(8,128)(2,1)S(1)} %get-tuple-element.60.refs_0_), channel_id=1, source_target_pairs={{0,2},{1,3},{2,0},{3,1},{4,6},{5,7},{6,4},{7,5},{8,10},{9,11},{10,... | collective-permute-start | bytes 393224 | tf_op jit(solution)/shard_map/ppermute | solution.py:360
  16.8 7.5 %collective-permute-start.4 = (bf16[8,16,512]{2,1,0:T(8,128)(2,1)S(1)}, bf16[8,16,512]{2,1,0:T(8,128)(2,1)S(1)}, u32[]{:S(2)}, u32[]{:S(2)}) collective-permute-start(bf16[8,16,512]{2,1,0:T(8,128)(2,1)S(1)} %get-tuple-element.60.refs_0_), channel_id=1, source_target_pairs={{0,3},{1,2},{2,1},{3,0},{4,7},{5,6},{6,5},{7,4},{8,11},{9,10},{10,... | collective-permute-start | bytes 393224 | tf_op jit(solution)/shard_map/ppermute | solution.py:360
  17.4 1.3 %collective-permute-start.7 = (bf16[4,2,16,256]{3,2,1,0:T(8,128)(2,1)S(1)}, bf16[4,2,16,256]{3,2,1,0:T(8,128)(2,1)S(1)}, u32[]{:S(2)}, u32[]{:S(2)}) collective-permute-start(bf16[4,2,16,256]{3,2,1,0:T(8,128)(2,1)S(1)} %get-tuple-element.52.after.refs_0_), channel_id=1, source_target_pairs={{0,8},{8,0},{16,24},{24,16},{1,9},{9,1},{17,25},{25,17},{2,10},{10... | collective-permute-start | bytes 196616 | tf_op jit(solution)/shard_map/ppermute | solution.py:269
  17.4 2.8 %collective-permute-start.9 = (bf16[4,2,16,256]{3,2,1,0:T(8,128)(2,1)S(1)}, bf16[4,2,16,256]{3,2,1,0:T(8,128)(2,1)S(1)}, u32[]{:S(2)}, u32[]{:S(2)}) collective-permute-start(bf16[4,2,16,256]{3,2,1,0:T(8,128)(2,1)S(1)} %collective-permute-done.8.refs_2_), channel_id=1, source_target_pairs={{0,8},{8,0},{16,24},{24,16},{1,9},{9,1},{17,25},{25,17},{2,10},{10... | collective-permute-start | bytes 196616 | tf_op jit(solution)/shard_map/ppermute | solution.py:269
  18.6 7.6 %collective-permute-start.13 = (bf16[8,16,384]{2,1,0:T(8,128)(2,1)S(1)}, bf16[8,16,384]{2,1,0:T(8,128)(2,1)S(1)}, u32[]{:S(2)}, u32[]{:S(2)}) collective-permute-start(bf16[8,16,384]{2,1,0:T(8,128)(2,1)S(1)} %get-tuple-element.65.refs_0_.refs_4_), channel_id=1, source_target_pairs={{0,1},{1,0},{2,3},{3,2},{4,5},{5,4},{6,7},{7,6},{8,9},{9,8},{10,11... | collective-permute-start | bytes 294920 | tf_op jit(solution)/shard_map/ppermute | solution.py:360
  20.2 6.3 %collective-permute-start.12 = (bf16[8,16,384]{2,1,0:T(8,128)(2,1)S(1)}, bf16[8,16,384]{2,1,0:T(8,128)(2,1)S(1)}, u32[]{:S(2)}, u32[]{:S(2)}) collective-permute-start(bf16[8,16,384]{2,1,0:T(8,128)(2,1)S(1)} %get-tuple-element.65.refs_0_.refs_4_), channel_id=1, source_target_pairs={{0,2},{1,3},{2,0},{3,1},{4,6},{5,7},{6,4},{7,5},{8,10},{9,11},{10,... | collective-permute-start | bytes 294920 | tf_op jit(solution)/shard_map/ppermute | solution.py:360
  21.5 6.2 %collective-permute-start.11 = (bf16[8,16,384]{2,1,0:T(8,128)(2,1)S(1)}, bf16[8,16,384]{2,1,0:T(8,128)(2,1)S(1)}, u32[]{:S(2)}, u32[]{:S(2)}) collective-permute-start(bf16[8,16,384]{2,1,0:T(8,128)(2,1)S(1)} %get-tuple-element.65.refs_0_.refs_4_), channel_id=1, source_target_pairs={{0,3},{1,2},{2,1},{3,0},{4,7},{5,6},{6,5},{7,4},{8,11},{9,10},{10,... | collective-permute-start | bytes 294920 | tf_op jit(solution)/shard_map/ppermute | solution.py:360
  25.0 7.1 %collective-permute-start.10 = (bf16[512,256]{1,0:T(8,128)(2,1)S(1)}, bf16[512,256]{1,0:T(8,128)(2,1)S(1)}, u32[]{:S(2)}, u32[]{:S(2)}) collective-permute-start(bf16[512,256]{1,0:T(8,128)(2,1)S(1)} %get-tuple-element.64.refs_8_), channel_id=1, source_target_pairs={{0,16},{8,24},{16,0},{24,8},{1,17},{9,25},{17,1},{25,9},{2,18},{10... | collective-permute-start | bytes 786440 | tf_op jit(solution)/shard_map/ppermute | solution.py:269
  28.7 10.3 %collective-permute-start.17 = (bf16[896,256]{1,0:T(8,128)(2,1)S(1)}, bf16[896,256]{1,0:T(8,128)(2,1)S(1)}, u32[]{:S(2)}, u32[]{:S(2)}) collective-permute-start(bf16[896,256]{1,0:T(8,128)(2,1)S(1)} %get-tuple-element.74.refs_0_), channel_id=1, source_target_pairs={{0,8},{8,0},{16,24},{24,16},{1,9},{9,1},{17,25},{25,17},{2,10},{10... | collective-permute-start | bytes 1376264 | tf_op jit(solution)/shard_map/ppermute | solution.py:269
  28.8 2.0 %collective-permute-start.14 = (bf16[2,4,2,16,256]{4,3,2,1,0:T(8,128)(2,1)S(1)}, bf16[2,4,2,16,256]{4,3,2,1,0:T(8,128)(2,1)S(1)}, u32[]{:S(2)}, u32[]{:S(2)}) collective-permute-start(bf16[2,4,2,16,256]{4,3,2,1,0:T(8,128)(2,1)S(1)} %get-tuple-element.68), channel_id=1, source_target_pairs={{0,8},{8,0},{16,24},{24,16},{1,9},{9,1},{17,25},{25,17},{2,10},{10... | collective-permute-start | bytes 393224 | tf_op jit(solution)/shard_map/ppermute | solution.py:269
  29.3 7.6 %collective-permute-start.16 = (bf16[384,256]{1,0:T(8,128)(2,1)S(1)}, bf16[384,256]{1,0:T(8,128)(2,1)S(1)}, u32[]{:S(2)}, u32[]{:S(2)}) collective-permute-start(bf16[384,256]{1,0:T(8,128)(2,1)S(1)} %get-tuple-element.66.refs_9_), channel_id=1, source_target_pairs={{0,16},{8,24},{16,0},{24,8},{1,17},{9,25},{17,1},{25,9},{2,18},{10... | collective-permute-start | bytes 589832 | tf_op jit(solution)/shard_map/ppermute | solution.py:269
  30.8 6.8 %collective-permute-start.15 = (bf16[1,4,2,16,256]{4,3,2,1,0:T(8,128)(2,1)S(1)}, bf16[1,4,2,16,256]{4,3,2,1,0:T(8,128)(2,1)S(1)}, u32[]{:S(2)}, u32[]{:S(2)}) collective-permute-start(bf16[1,4,2,16,256]{4,3,2,1,0:T(8,128)(2,1)S(1)} %get-tuple-element.71), channel_id=1, source_target_pairs={{0,16},{8,24},{16,0},{24,8},{1,17},{9,25},{17,1},{25,9},{2,18},{10... | collective-permute-start | bytes 196616 | tf_op jit(solution)/shard_map/ppermute | solution.py:269
  32.1 6.9 %collective-permute-start.18 = (bf16[512,256]{1,0:T(8,128)(2,1)S(1)}, bf16[512,256]{1,0:T(8,128)(2,1)S(1)}, u32[]{:S(2)}, u32[]{:S(2)}) collective-permute-start(bf16[512,256]{1,0:T(8,128)(2,1)S(1)} %collective-permute-done.10.refs_1_), channel_id=1, source_target_pairs={{0,8},{8,0},{16,24},{24,16},{1,9},{9,1},{17,25},{25,17},{2,10},{10... | collective-permute-start | bytes 786440 | tf_op jit(solution)/shard_map/ppermute | solution.py:269
  33.7 3.9 %copy-start = (bf16[1,128,256]{2,1,0:T(8,128)(2,1)S(1)}, bf16[1,128,256]{2,1,0:T(8,128)(2,1)}, u32[]{:S(2)}) copy-start(bf16[1,128,256]{2,1,0:T(8,128)(2,1)} %gate.1) | copy-start | bytes 196612
  33.7 3.9 %copy-start.1 = (bf16[1,128,256]{2,1,0:T(8,128)(2,1)S(1)}, bf16[1,128,256]{2,1,0:T(8,128)(2,1)}, u32[]{:S(2)}) copy-start(bf16[1,128,256]{2,1,0:T(8,128)(2,1)} %up.1) | copy-start | bytes 196612
  37.6 1.4 %collective-permute-start.19 = (bf16[384,256]{1,0:T(8,128)(2,1)S(1)}, bf16[384,256]{1,0:T(8,128)(2,1)S(1)}, u32[]{:S(2)}, u32[]{:S(2)}) collective-permute-start(bf16[384,256]{1,0:T(8,128)(2,1)S(1)} %collective-permute-done.16.refs_2_), channel_id=1, source_target_pairs={{0,8},{8,0},{16,24},{24,16},{1,9},{9,1},{17,25},{25,17},{2,10},{10... | collective-permute-start | bytes 589832 | tf_op jit(solution)/shard_map/ppermute | solution.py:269
where the time goes:
time: 40.2 us; the launch traced here: 40.1 us
  starting transfers between devices  18.9 us (47%)
  waiting for transfers between devices  11.4 us (28%)
  Pallas kernels  8.93 us (22%)
  between operations  0.76 us (2%)
    ppermute x6, starting transfers between devices, local(): lax.ppermute(piece, 'expert', [(k, k ^ d) for k in range(sources)])  7.04 us
    ppermute x11, starting transfers between devices, over_dp(): return lax.ppermute(x, 'dp', [(i, i ^ d) for i in range(pieces)])  6.26 us
    ppermute x3, starting transfers between devices, local(): blocks[n] = lax.ppermute(blocks[n], ('dp', 'expert'), pairs)  5.64 us
    ppermute x11, waiting for transfers between devices, over_dp(): return lax.ppermute(x, 'dp', [(i, i ^ d) for i in range(pieces)])  4.71 us
    ppermute x6, waiting for transfers between devices, local(): lax.ppermute(piece, 'expert', [(k, k ^ d) for k in range(sources)])  3.64 us
    ppermute x3, waiting for transfers between devices, local(): blocks[n] = lax.ppermute(blocks[n], ('dp', 'expert'), pairs)  3.05 us
    pallas_call x2, Pallas kernels, join(): pl.pallas_call(functools.partial(join_kernel, high, [entry[:3] for entry...  1.9 us
    pallas_call x1, Pallas kernels, local(): pl.pallas_call(fetch_kernel, out_shape=[shape((high, across), f32)] * 3,...  1.76 us
  transfers between devices with their start and end apart: 20, of which 10 were waited for; matrix products, arithmetic and copies ran while one was open for 0% of the time, Pallas kernels for 17%

commit v1 on v0

--- a/solution.py
+++ b/solution.py
@@ -42,7 +42,9 @@
 
 
 def turns(ways):
-    return [0, *range(ways - 1, 0, -1)]
+    near = [d for d in range(1, ways) if d & (d - 1) == 0]
+    far = [d for d in range(1, ways) if d & (d - 1)]
+    return [0, *near[1:], *far, *near[:1]]
 
 
 def seat_of(ways):

time: 40.2 us -> 40.2 us (level)
  starting transfers between devices: 18.9 us -> 19.7 us
  waiting for transfers between devices: 11.4 us -> 10.6 us
    ppermute x6, waiting for transfers between devices: 3.64 us -> 2.88 us  [local(): lax.ppermute(piece, 'expert', [(k, k ^ d) for k in range(sources)])]
    ppermute x6, starting transfers between devices: 7.04 us -> 7.74 us  [local(): lax.ppermute(piece, 'expert', [(k, k ^ d) for k in range(sources)])]
where the time goes in v1:
time: 40.2 us; the launch traced here: 40.1 us
  starting transfers between devices  19.7 us (49%)
  waiting for transfers between devices  10.6 us (26%)
  Pallas kernels  8.93 us (22%)
  between operations  0.76 us (2%)
    ppermute x6, starting transfers between devices, local(): lax.ppermute(piece, 'expert', [(k, k ^ d) for k in range(sources)])  7.74 us
    ppermute x11, starting transfers between devices, over_dp(): return lax.ppermute(x, 'dp', [(i, i ^ d) for i in range(pieces)])  6.33 us
    ppermute x3, starting transfers between devices, local(): blocks[n] = lax.ppermute(blocks[n], ('dp', 'expert'), pairs)  5.64 us
    ppermute x11, waiting for transfers between devices, over_dp(): return lax.ppermute(x, 'dp', [(i, i ^ d) for i in range(pieces)])  4.7 us
    ppermute x3, waiting for transfers between devices, local(): blocks[n] = lax.ppermute(blocks[n], ('dp', 'expert'), pairs)  3.05 us
    ppermute x6, waiting for transfers between devices, local(): lax.ppermute(piece, 'expert', [(k, k ^ d) for k in range(sources)])  2.88 us
    pallas_call x2, Pallas kernels, join(): pl.pallas_call(functools.partial(join_kernel, high, [entry[:3] for entry...  1.9 us
    pallas_call x1, Pallas kernels, local(): pl.pallas_call(fetch_kernel, out_shape=[shape((high, across), f32)] * 3,...  1.76 us
  transfers between devices with their start and end apart: 20, of which 10 were waited for; matrix products, arithmetic and copies ran while one was open for 0% of the time, Pallas kernels for 17%

profile of v1, /device:TPU:0, one launch (start us, length us, event | category | flops | bytes accessed | tf_op | source)
XLA Modules:
  0.0 40.1 jit_solution(10791240611426965157)
XLA Ops:
  0.6 1.2 %scale.1 = (bf16[4,2,16,256]{3,2,1,0:T(8,128)(2,1)S(1)}, bf16[2,16,896]{2,1,0:T(8,128)(2,1)S(1)}, bf16[2,16,896]{2,1,0:T(8,128)(2,1)S(1)}, bf16[2,16,896]{2,1,0:T(8,128)(2,1)S(1)}, bf16[2,16,896]{2,1,0:T(8,128)(2,1)S(1)}) custom-call(s32[1,2]{1,0:T(1,128)} %counts_in.1, f32[1,2,16]{2,1,0:T(2,128)} %router_in.1, bf16[1,2,16,3584]{3,2,1,0:T(8,128)(2,1)} %rows_in.1, ...), custom_call_target="tpu_custom_call" | custom-call | tf_op jit(solution)/shard_map/scale/pallas_call | solution.py:277
  1.9 4.1 %collective-permute-start = (bf16[2,16,896]{2,1,0:T(8,128)(2,1)S(1)}, bf16[2,16,896]{2,1,0:T(8,128)(2,1)S(1)}, u32[]{:S(2)}, u32[]{:S(2)}) collective-permute-start(bf16[2,16,896]{2,1,0:T(8,128)(2,1)S(1)} %get-tuple-element.48), channel_id=1, source_target_pairs={{0,4},{1,5},{2,6},{3,7},{4,0},{5,1},{6,2},{7,3},{8,12},{9,13},{10,... | collective-permute-start | bytes 172040 | tf_op jit(solution)/shard_map/ppermute | solution.py:309
  6.0 1.3 %collective-permute-start.1 = (bf16[2,16,896]{2,1,0:T(8,128)(2,1)S(1)}, bf16[2,16,896]{2,1,0:T(8,128)(2,1)S(1)}, u32[]{:S(2)}, u32[]{:S(2)}) collective-permute-start(bf16[2,16,896]{2,1,0:T(8,128)(2,1)S(1)} %get-tuple-element.49), channel_id=1, source_target_pairs={{0,20},{1,21},{2,22},{3,23},{4,16},{5,17},{6,18},{7,19},{8,28},{9,... | collective-permute-start | bytes 172040 | tf_op jit(solution)/shard_map/ppermute | solution.py:309
  7.2 0.3 collective-permute-start.2
  7.5 1.8 %fetch.1 = (f32[896,256]{1,0:T(8,128)S(1)}, f32[896,256]{1,0:T(8,128)S(1)}, f32[896,256]{1,0:T(8,128)S(1)}) custom-call(bf16[4,2,16,256]{3,2,1,0:T(8,128)(2,1)S(1)} %get-tuple-element.52.after.refs_0_, f32[896,256]{1,0:T(8,128)} %refs_0_.1, f32[896,256]{1,0:T(8,128)} %refs_1_.1, f32[896,256]{1,0:T(8,128)} %refs_2_.1), custom_call_target="tpu_custom_call" | custom-call | bytes 5505024 | tf_op jit(solution)/shard_map/fetch/pallas_call | solution.py:310
  9.3 0.0 collective-permute-done.refs_0_.refs_2_
  9.3 3.0 %collective-permute-done.1.refs_1_.refs_3_ = bf16[2,16,896]{2,1,0:T(8,128)(2,1)S(1)} collective-permute-done((bf16[2,16,896]{2,1,0:T(8,128)(2,1)S(1)}, bf16[2,16,896]{2,1,0:T(8,128)(2,1)S(1)}, u32[]{:S(2)}, u32[]{:S(2)}) %collective-permute-start.1) | collective-permute-done | bytes 57376 | tf_op jit(solution)/shard_map/ppermute | solution.py:309
  12.3 0.0 collective-permute-done.2.refs_2_.refs_1_
  12.3 0.1 collective-permute-start.3
  12.4 1.4 %collective-permute-start.8 = (bf16[4,2,16,256]{3,2,1,0:T(8,128)(2,1)S(1)}, bf16[4,2,16,256]{3,2,1,0:T(8,128)(2,1)S(1)}, u32[]{:S(2)}, u32[]{:S(2)}) collective-permute-start(bf16[4,2,16,256]{3,2,1,0:T(8,128)(2,1)S(1)} %get-tuple-element.52.after.refs_0_), channel_id=1, source_target_pairs={{0,16},{8,24},{16,0},{24,8},{1,17},{9,25},{17,1},{25,9},{2,18},{10... | collective-permute-start | bytes 196616 | tf_op jit(solution)/shard_map/ppermute | solution.py:271
  13.8 0.0 collective-permute-done.3.other
  13.8 1.6 %collective-permute-start.6 = (bf16[8,16,512]{2,1,0:T(8,128)(2,1)S(1)}, bf16[8,16,512]{2,1,0:T(8,128)(2,1)S(1)}, u32[]{:S(2)}, u32[]{:S(2)}) collective-permute-start(bf16[8,16,512]{2,1,0:T(8,128)(2,1)S(1)} %get-tuple-element.60.refs_0_), channel_id=1, source_target_pairs={{0,1},{1,0},{2,3},{3,2},{4,5},{5,4},{6,7},{7,6},{8,9},{9,8},{10,11... | collective-permute-start | bytes 393224 | tf_op jit(solution)/shard_map/ppermute | solution.py:362
  15.4 1.3 %collective-permute-start.5 = (bf16[8,16,512]{2,1,0:T(8,128)(2,1)S(1)}, bf16[8,16,512]{2,1,0:T(8,128)(2,1)S(1)}, u32[]{:S(2)}, u32[]{:S(2)}) collective-permute-start(bf16[8,16,512]{2,1,0:T(8,128)(2,1)S(1)} %get-tuple-element.60.refs_0_), channel_id=1, source_target_pairs={{0,3},{1,2},{2,1},{3,0},{4,7},{5,6},{6,5},{7,4},{8,11},{9,10},{10,... | collective-permute-start | bytes 393224 | tf_op jit(solution)/shard_map/ppermute | solution.py:362
  16.7 0.7 %collective-permute-start.4 = (bf16[8,16,512]{2,1,0:T(8,128)(2,1)S(1)}, bf16[8,16,512]{2,1,0:T(8,128)(2,1)S(1)}, u32[]{:S(2)}, u32[]{:S(2)}) collective-permute-start(bf16[8,16,512]{2,1,0:T(8,128)(2,1)S(1)} %get-tuple-element.60.refs_0_), channel_id=1, source_target_pairs={{0,2},{1,3},{2,0},{3,1},{4,6},{5,7},{6,4},{7,5},{8,10},{9,11},{10,... | collective-permute-start | bytes 393224 | tf_op jit(solution)/shard_map/ppermute | solution.py:362
  17.4 0.0 collective-permute-start.7
  17.4 0.0 collective-permute-done.8.refs_2_
  17.4 0.5 %collective-permute-start.9 = (bf16[4,2,16,256]{3,2,1,0:T(8,128)(2,1)S(1)}, bf16[4,2,16,256]{3,2,1,0:T(8,128)(2,1)S(1)}, u32[]{:S(2)}, u32[]{:S(2)}) collective-permute-start(bf16[4,2,16,256]{3,2,1,0:T(8,128)(2,1)S(1)} %collective-permute-done.8.refs_2_), channel_id=1, source_target_pairs={{0,8},{8,0},{16,24},{24,16},{1,9},{9,1},{17,25},{25,17},{2,10},{10... | collective-permute-start | bytes 196616 | tf_op jit(solution)/shard_map/ppermute | solution.py:271
  17.9 0.7 %collective-permute-done.7.refs_1_ = bf16[4,2,16,256]{3,2,1,0:T(8,128)(2,1)S(1)} collective-permute-done((bf16[4,2,16,256]{3,2,1,0:T(8,128)(2,1)S(1)}, bf16[4,2,16,256]{3,2,1,0:T(8,128)(2,1)S(1)}, u32[]{:S(2)}, u32[]{:S(2)}) %collective-permute-start.7) | collective-permute-done | bytes 65568 | tf_op jit(solution)/shard_map/ppermute | solution.py:271
  18.6 1.5 %collective-permute-start.13 = (bf16[8,16,384]{2,1,0:T(8,128)(2,1)S(1)}, bf16[8,16,384]{2,1,0:T(8,128)(2,1)S(1)}, u32[]{:S(2)}, u32[]{:S(2)}) collective-permute-start(bf16[8,16,384]{2,1,0:T(8,128)(2,1)S(1)} %get-tuple-element.65.refs_0_.refs_4_), channel_id=1, source_target_pairs={{0,1},{1,0},{2,3},{3,2},{4,5},{5,4},{6,7},{7,6},{8,9},{9,8},{10,11... | collective-permute-start | bytes 294920 | tf_op jit(solution)/shard_map/ppermute | solution.py:362
  20.2 0.0 collective-permute-done.9.refs_3_
  20.2 1.3 %collective-permute-start.12 = (bf16[8,16,384]{2,1,0:T(8,128)(2,1)S(1)}, bf16[8,16,384]{2,1,0:T(8,128)(2,1)S(1)}, u32[]{:S(2)}, u32[]{:S(2)}) collective-permute-start(bf16[8,16,384]{2,1,0:T(8,128)(2,1)S(1)} %get-tuple-element.65.refs_0_.refs_4_), channel_id=1, source_target_pairs={{0,3},{1,2},{2,1},{3,0},{4,7},{5,6},{6,5},{7,4},{8,11},{9,10},{10,... | collective-permute-start | bytes 294920 | tf_op jit(solution)/shard_map/ppermute | solution.py:362
  21.5 0.7 %collective-permute-done.6.refs_3_ = bf16[8,16,512]{2,1,0:T(8,128)(2,1)S(1)} collective-permute-done((bf16[8,16,512]{2,1,0:T(8,128)(2,1)S(1)}, bf16[8,16,512]{2,1,0:T(8,128)(2,1)S(1)}, u32[]{:S(2)}, u32[]{:S(2)}) %collective-permute-start.6) | collective-permute-done | bytes 131104 | tf_op jit(solution)/shard_map/ppermute | solution.py:362
  22.2 1.4 %collective-permute-start.11 = (bf16[8,16,384]{2,1,0:T(8,128)(2,1)S(1)}, bf16[8,16,384]{2,1,0:T(8,128)(2,1)S(1)}, u32[]{:S(2)}, u32[]{:S(2)}) collective-permute-start(bf16[8,16,384]{2,1,0:T(8,128)(2,1)S(1)} %get-tuple-element.65.refs_0_.refs_4_), channel_id=1, source_target_pairs={{0,2},{1,3},{2,0},{3,1},{4,6},{5,7},{6,4},{7,5},{8,10},{9,11},{10,... | collective-permute-start | bytes 294920 | tf_op jit(solution)/shard_map/ppermute | solution.py:362
  23.5 0.0 collective-permute-done.5.refs_2_
  23.6 0.7 %collective-permute-done.4.refs_1_ = bf16[8,16,512]{2,1,0:T(8,128)(2,1)S(1)} collective-permute-done((bf16[8,16,512]{2,1,0:T(8,128)(2,1)S(1)}, bf16[8,16,512]{2,1,0:T(8,128)(2,1)S(1)}, u32[]{:S(2)}, u32[]{:S(2)}) %collective-permute-start.4) | collective-permute-done | bytes 131104 | tf_op jit(solution)/shard_map/ppermute | solution.py:362
  24.2 0.7 %update.2 = (bf16[512,256]{1,0:T(8,128)(2,1)S(1)}, f32[512,256]{1,0:T(8,128)S(1)}, f32[512,256]{1,0:T(8,128)S(1)}, f32[512,256]{1,0:T(8,128)S(1)}) custom-call(bf16[8,16,512]{2,1,0:T(8,128)(2,1)S(1)} %get-tuple-element.60.refs_0_, bf16[8,16,512]{2,1,0:T(8,128)(2,1)S(1)} %collective-permute-done.4.refs_1_, ...), custom_call_target="tpu_custom_call" | custom-call | flops 134217728 | bytes 5963776 | tf_op jit(solution)/shard_map/update/pallas_call | solution.py:369
  24.9 1.3 %collective-permute-start.10 = (bf16[512,256]{1,0:T(8,128)(2,1)S(1)}, bf16[512,256]{1,0:T(8,128)(2,1)S(1)}, u32[]{:S(2)}, u32[]{:S(2)}) collective-permute-start(bf16[512,256]{1,0:T(8,128)(2,1)S(1)} %get-tuple-element.64.refs_8_), channel_id=1, source_target_pairs={{0,16},{8,24},{16,0},{24,8},{1,17},{9,25},{17,1},{25,9},{2,18},{10... | collective-permute-start | bytes 786440 | tf_op jit(solution)/shard_map/ppermute | solution.py:271
  26.2 0.0 collective-permute-done.13.refs_3_.refs_7_
  26.2 1.2 %collective-permute-done.12.refs_2_.refs_6_ = bf16[8,16,384]{2,1,0:T(8,128)(2,1)S(1)} collective-permute-done((bf16[8,16,384]{2,1,0:T(8,128)(2,1)S(1)}, bf16[8,16,384]{2,1,0:T(8,128)(2,1)S(1)}, u32[]{:S(2)}, u32[]{:S(2)}) %collective-permute-start.12) | collective-permute-done | bytes 98336 | tf_op jit(solution)/shard_map/ppermute | solution.py:362
  27.4 0.3 collective-permute-done.11.refs_1_.refs_5_
  27.7 0.6 %update.3 = (bf16[384,256]{1,0:T(8,128)(2,1)S(1)}, f32[384,256]{1,0:T(8,128)S(1)}, f32[384,256]{1,0:T(8,128)S(1)}, f32[384,256]{1,0:T(8,128)S(1)}) custom-call(bf16[8,16,384]{2,1,0:T(8,128)(2,1)S(1)} %get-tuple-element.65.refs_0_.refs_4_, bf16[8,16,384]{2,1,0:T(8,128)(2,1)S(1)} %collective-permute-done.11.refs_1_.refs_5_, ...), custom_call_target="tpu_custom_call" | custom-call | flops 100663296 | bytes 5963776 | tf_op jit(solution)/shard_map/update/pallas_call | solution.py:369
  28.3 0.4 %partial.1 = (f32[2,4,2,16,256]{4,3,2,1,0:T(8,128)S(1)}, bf16[2,4,2,16,256]{4,3,2,1,0:T(8,128)(2,1)S(1)}, bf16[896,256]{1,0:T(8,128)(2,1)S(1)}) custom-call(bf16[8,16,512]{2,1,0:T(8,128)(2,1)S(1)} %get-tuple-element.60.refs_0_, bf16[8,16,512]{2,1,0:T(8,128)(2,1)S(1)} %collective-permute-done.4.refs_1_, ...), custom_call_target="tpu_custom_call" | custom-call | flops 234881024 | bytes 2752512 | tf_op jit(solution)/shard_map/partial/pallas_call | solution.py:387
  28.7 0.1 collective-permute-start.17
  28.8 0.5 %collective-permute-start.14 = (bf16[2,4,2,16,256]{4,3,2,1,0:T(8,128)(2,1)S(1)}, bf16[2,4,2,16,256]{4,3,2,1,0:T(8,128)(2,1)S(1)}, u32[]{:S(2)}, u32[]{:S(2)}) collective-permute-start(bf16[2,4,2,16,256]{4,3,2,1,0:T(8,128)(2,1)S(1)} %get-tuple-element.68), channel_id=1, source_target_pairs={{0,8},{8,0},{16,24},{24,16},{1,9},{9,1},{17,25},{25,17},{2,10},{10... | collective-permute-start | bytes 393224 | tf_op jit(solution)/shard_map/ppermute | solution.py:271
  29.3 1.2 %collective-permute-start.16 = (bf16[384,256]{1,0:T(8,128)(2,1)S(1)}, bf16[384,256]{1,0:T(8,128)(2,1)S(1)}, u32[]{:S(2)}, u32[]{:S(2)}) collective-permute-start(bf16[384,256]{1,0:T(8,128)(2,1)S(1)} %get-tuple-element.66.refs_9_), channel_id=1, source_target_pairs={{0,16},{8,24},{16,0},{24,8},{1,17},{9,25},{17,1},{25,9},{2,18},{10... | collective-permute-start | bytes 589832 | tf_op jit(solution)/shard_map/ppermute | solution.py:271
  30.5 0.3 collective-permute-done.14.arrived
  30.8 1.3 %collective-permute-start.15 = (bf16[1,4,2,16,256]{4,3,2,1,0:T(8,128)(2,1)S(1)}, bf16[1,4,2,16,256]{4,3,2,1,0:T(8,128)(2,1)S(1)}, u32[]{:S(2)}, u32[]{:S(2)}) collective-permute-start(bf16[1,4,2,16,256]{4,3,2,1,0:T(8,128)(2,1)S(1)} %get-tuple-element.71), channel_id=1, source_target_pairs={{0,16},{8,24},{16,0},{24,8},{1,17},{9,25},{17,1},{25,9},{2,18},{10... | collective-permute-start | bytes 196616 | tf_op jit(solution)/shard_map/ppermute | solution.py:271
  32.1 0.0 collective-permute-done.10.refs_1_
  32.1 0.0 collective-permute-start.18
  32.1 1.6 %store.1 = (f32[896,256]{1,0:T(8,128)}, f32[896,256]{1,0:T(8,128)}, f32[896,256]{1,0:T(8,128)}) custom-call(f32[512,256]{1,0:T(8,128)S(1)} %get-tuple-element.76.refs_0_, f32[512,256]{1,0:T(8,128)S(1)} %get-tuple-element.77.refs_1_, f32[512,256]{1,0:T(8,128)S(1)} %get-tuple-element.78.refs_2_, f32[384,256]{1,0:T(8,128)S(1)} %get-tuple-element.79.refs_3_, ...), custom_call_target="tpu_custom_call" | custom-call | bytes 5505024 | tf_op jit(solution)/shard_map/store/pallas_call | solution.py:430
  33.7 0.0 copy-start
  33.7 0.0 copy-start.1
  33.7 0.9 %join.2.refs_4_ = bf16[3584,256]{1,0:T(8,128)(2,1)} custom-call(bf16[896,256]{1,0:T(8,128)(2,1)S(1)} %get-tuple-element.74.refs_0_, bf16[512,256]{1,0:T(8,128)(2,1)S(1)} %collective-permute-done.10.refs_1_), custom_call_target="tpu_custom_call" | custom-call | tf_op jit(solution)/shard_map/join/pallas_call | solution.py:442
  34.6 2.3 %collective-permute-done.16.refs_2_ = bf16[384,256]{1,0:T(8,128)(2,1)S(1)} collective-permute-done((bf16[384,256]{1,0:T(8,128)(2,1)S(1)}, bf16[384,256]{1,0:T(8,128)(2,1)S(1)}, u32[]{:S(2)}, u32[]{:S(2)}) %collective-permute-start.16) | collective-permute-done | bytes 196640 | tf_op jit(solution)/shard_map/ppermute | solution.py:271
  36.9 0.7 %collective-permute-done.15.arrived = bf16[1,4,2,16,256]{4,3,2,1,0:T(8,128)(2,1)S(1)} collective-permute-done((bf16[1,4,2,16,256]{4,3,2,1,0:T(8,128)(2,1)S(1)}, bf16[1,4,2,16,256]{4,3,2,1,0:T(8,128)(2,1)S(1)}, u32[]{:S(2)}, u32[]{:S(2)}) %collective-permute-start.15) | collective-permute-done | bytes 65568 | tf_op jit(solution)/shard_map/ppermute | solution.py:271
  37.6 0.0 collective-permute-start.19
  37.6 0.0 copy-done
  37.6 0.0 copy-done.1
  37.6 0.7 %gates.1 = (bf16[1,128,256]{2,1,0:T(8,128)(2,1)}, bf16[1,128,256]{2,1,0:T(8,128)(2,1)}) custom-call(bf16[1,128,256]{2,1,0:T(8,128)(2,1)S(1)} %copy-done, bf16[1,128,256]{2,1,0:T(8,128)(2,1)S(1)} %copy-done.1, f32[1,4,2,16,256]{4,3,2,1,0:T(8,128)S(1)} %get-tuple-element.70.held, bf16[1,4,2,16,256]{4,3,2,1,0:T(8,128)(2,1)S(1)} %collective-permute-done.15.arrived), custom_call_target="tpu_custom_call" | custom-call | tf_op jit(solution)/shard_map/gates/pallas_call | solution.py:421
  38.3 0.7 %collective-permute-done.19.refs_3_ = bf16[384,256]{1,0:T(8,128)(2,1)S(1)} collective-permute-done((bf16[384,256]{1,0:T(8,128)(2,1)S(1)}, bf16[384,256]{1,0:T(8,128)(2,1)S(1)}, u32[]{:S(2)}, u32[]{:S(2)}) %collective-permute-start.19) | collective-permute-done | bytes 196640 | tf_op jit(solution)/shard_map/ppermute | solution.py:271
  39.0 0.0 collective-permute-done.17.refs_0_
  39.0 0.0 collective-permute-done.18.refs_1_
  39.0 1.0 %join.3 = bf16[3584,256]{1,0:T(8,128)(2,1)} custom-call(bf16[896,256]{1,0:T(8,128)(2,1)S(1)} %collective-permute-done.17.refs_0_, bf16[512,256]{1,0:T(8,128)(2,1)S(1)} %collective-permute-done.18.refs_1_, bf16[384,256]{1,0:T(8,128)(2,1)S(1)} %collective-permute-done.16.refs_2_, ...), custom_call_target="tpu_custom_call", output_to_operand_aliasing={{}: (4, {})} | custom-call | tf_op jit(solution)/shard_map/join/pallas_call | solution.py:442
  (4 shorter events, 0.1 us)
Async XLA Ops:
  1.9 7.4 %collective-permute-start = (bf16[2,16,896]{2,1,0:T(8,128)(2,1)S(1)}, bf16[2,16,896]{2,1,0:T(8,128)(2,1)S(1)}, u32[]{:S(2)}, u32[]{:S(2)}) collective-permute-start(bf16[2,16,896]{2,1,0:T(8,128)(2,1)S(1)} %get-tuple-element.48), channel_id=1, source_target_pairs={{0,4},{1,5},{2,6},{3,7},{4,0},{5,1},{6,2},{7,3},{8,12},{9,13},{10,... | collective-permute-start | bytes 172040 | tf_op jit(solution)/shard_map/ppermute | solution.py:309
  6.0 6.4 %collective-permute-start.1 = (bf16[2,16,896]{2,1,0:T(8,128)(2,1)S(1)}, bf16[2,16,896]{2,1,0:T(8,128)(2,1)S(1)}, u32[]{:S(2)}, u32[]{:S(2)}) collective-permute-start(bf16[2,16,896]{2,1,0:T(8,128)(2,1)S(1)} %get-tuple-element.49), channel_id=1, source_target_pairs={{0,20},{1,21},{2,22},{3,23},{4,16},{5,17},{6,18},{7,19},{8,28},{9,... | collective-permute-start | bytes 172040 | tf_op jit(solution)/shard_map/ppermute | solution.py:309
  7.2 5.1 %collective-permute-start.2 = (bf16[2,16,896]{2,1,0:T(8,128)(2,1)S(1)}, bf16[2,16,896]{2,1,0:T(8,128)(2,1)S(1)}, u32[]{:S(2)}, u32[]{:S(2)}) collective-permute-start(bf16[2,16,896]{2,1,0:T(8,128)(2,1)S(1)} %get-tuple-element.50), channel_id=1, source_target_pairs={{0,16},{1,17},{2,18},{3,19},{4,20},{5,21},{6,22},{7,23},{8,24},{9,... | collective-permute-start | bytes 172040 | tf_op jit(solution)/shard_map/ppermute | solution.py:309
  12.3 1.5 %collective-permute-start.3 = (bf16[4,16,896]{2,1,0:T(8,128)(2,1)S(1)}, bf16[4,16,896]{2,1,0:T(8,128)(2,1)S(1)}, u32[]{:S(2)}, u32[]{:S(2)}) collective-permute-start(bf16[4,16,896]{2,1,0:T(8,128)(2,1)S(1)} %share.1), channel_id=1, source_target_pairs={{0,8},{8,0},{16,24},{24,16},{1,9},{9,1},{17,25},{25,17},{2,10},{10... | collective-permute-start | bytes 344072 | tf_op jit(solution)/shard_map/ppermute | solution.py:271
  12.4 5.0 %collective-permute-start.8 = (bf16[4,2,16,256]{3,2,1,0:T(8,128)(2,1)S(1)}, bf16[4,2,16,256]{3,2,1,0:T(8,128)(2,1)S(1)}, u32[]{:S(2)}, u32[]{:S(2)}) collective-permute-start(bf16[4,2,16,256]{3,2,1,0:T(8,128)(2,1)S(1)} %get-tuple-element.52.after.refs_0_), channel_id=1, source_target_pairs={{0,16},{8,24},{16,0},{24,8},{1,17},{9,25},{17,1},{25,9},{2,18},{10... | collective-permute-start | bytes 196616 | tf_op jit(solution)/shard_map/ppermute | solution.py:271
  13.8 8.3 %collective-permute-start.6 = (bf16[8,16,512]{2,1,0:T(8,128)(2,1)S(1)}, bf16[8,16,512]{2,1,0:T(8,128)(2,1)S(1)}, u32[]{:S(2)}, u32[]{:S(2)}) collective-permute-start(bf16[8,16,512]{2,1,0:T(8,128)(2,1)S(1)} %get-tuple-element.60.refs_0_), channel_id=1, source_target_pairs={{0,1},{1,0},{2,3},{3,2},{4,5},{5,4},{6,7},{7,6},{8,9},{9,8},{10,11... | collective-permute-start | bytes 393224 | tf_op jit(solution)/shard_map/ppermute | solution.py:362
  15.4 8.1 %collective-permute-start.5 = (bf16[8,16,512]{2,1,0:T(8,128)(2,1)S(1)}, bf16[8,16,512]{2,1,0:T(8,128)(2,1)S(1)}, u32[]{:S(2)}, u32[]{:S(2)}) collective-permute-start(bf16[8,16,512]{2,1,0:T(8,128)(2,1)S(1)} %get-tuple-element.60.refs_0_), channel_id=1, source_target_pairs={{0,3},{1,2},{2,1},{3,0},{4,7},{5,6},{6,5},{7,4},{8,11},{9,10},{10,... | collective-permute-start | bytes 393224 | tf_op jit(solution)/shard_map/ppermute | solution.py:362
  16.7 7.5 %collective-permute-start.4 = (bf16[8,16,512]{2,1,0:T(8,128)(2,1)S(1)}, bf16[8,16,512]{2,1,0:T(8,128)(2,1)S(1)}, u32[]{:S(2)}, u32[]{:S(2)}) collective-permute-start(bf16[8,16,512]{2,1,0:T(8,128)(2,1)S(1)} %get-tuple-element.60.refs_0_), channel_id=1, source_target_pairs={{0,2},{1,3},{2,0},{3,1},{4,6},{5,7},{6,4},{7,5},{8,10},{9,11},{10,... | collective-permute-start | bytes 393224 | tf_op jit(solution)/shard_map/ppermute | solution.py:362
  17.4 1.3 %collective-permute-start.7 = (bf16[4,2,16,256]{3,2,1,0:T(8,128)(2,1)S(1)}, bf16[4,2,16,256]{3,2,1,0:T(8,128)(2,1)S(1)}, u32[]{:S(2)}, u32[]{:S(2)}) collective-permute-start(bf16[4,2,16,256]{3,2,1,0:T(8,128)(2,1)S(1)} %get-tuple-element.52.after.refs_0_), channel_id=1, source_target_pairs={{0,8},{8,0},{16,24},{24,16},{1,9},{9,1},{17,25},{25,17},{2,10},{10... | collective-permute-start | bytes 196616 | tf_op jit(solution)/shard_map/ppermute | solution.py:271
  17.4 2.8 %collective-permute-start.9 = (bf16[4,2,16,256]{3,2,1,0:T(8,128)(2,1)S(1)}, bf16[4,2,16,256]{3,2,1,0:T(8,128)(2,1)S(1)}, u32[]{:S(2)}, u32[]{:S(2)}) collective-permute-start(bf16[4,2,16,256]{3,2,1,0:T(8,128)(2,1)S(1)} %collective-permute-done.8.refs_2_), channel_id=1, source_target_pairs={{0,8},{8,0},{16,24},{24,16},{1,9},{9,1},{17,25},{25,17},{2,10},{10... | collective-permute-start | bytes 196616 | tf_op jit(solution)/shard_map/ppermute | solution.py:271
  18.6 7.6 %collective-permute-start.13 = (bf16[8,16,384]{2,1,0:T(8,128)(2,1)S(1)}, bf16[8,16,384]{2,1,0:T(8,128)(2,1)S(1)}, u32[]{:S(2)}, u32[]{:S(2)}) collective-permute-start(bf16[8,16,384]{2,1,0:T(8,128)(2,1)S(1)} %get-tuple-element.65.refs_0_.refs_4_), channel_id=1, source_target_pairs={{0,1},{1,0},{2,3},{3,2},{4,5},{5,4},{6,7},{7,6},{8,9},{9,8},{10,11... | collective-permute-start | bytes 294920 | tf_op jit(solution)/shard_map/ppermute | solution.py:362
  20.2 7.2 %collective-permute-start.12 = (bf16[8,16,384]{2,1,0:T(8,128)(2,1)S(1)}, bf16[8,16,384]{2,1,0:T(8,128)(2,1)S(1)}, u32[]{:S(2)}, u32[]{:S(2)}) collective-permute-start(bf16[8,16,384]{2,1,0:T(8,128)(2,1)S(1)} %get-tuple-element.65.refs_0_.refs_4_), channel_id=1, source_target_pairs={{0,3},{1,2},{2,1},{3,0},{4,7},{5,6},{6,5},{7,4},{8,11},{9,10},{10,... | collective-permute-start | bytes 294920 | tf_op jit(solution)/shard_map/ppermute | solution.py:362
  22.2 5.6 %collective-permute-start.11 = (bf16[8,16,384]{2,1,0:T(8,128)(2,1)S(1)}, bf16[8,16,384]{2,1,0:T(8,128)(2,1)S(1)}, u32[]{:S(2)}, u32[]{:S(2)}) collective-permute-start(bf16[8,16,384]{2,1,0:T(8,128)(2,1)S(1)} %get-tuple-element.65.refs_0_.refs_4_), channel_id=1, source_target_pairs={{0,2},{1,3},{2,0},{3,1},{4,6},{5,7},{6,4},{7,5},{8,10},{9,11},{10,... | collective-permute-start | bytes 294920 | tf_op jit(solution)/shard_map/ppermute | solution.py:362
  24.9 7.2 %collective-permute-start.10 = (bf16[512,256]{1,0:T(8,128)(2,1)S(1)}, bf16[512,256]{1,0:T(8,128)(2,1)S(1)}, u32[]{:S(2)}, u32[]{:S(2)}) collective-permute-start(bf16[512,256]{1,0:T(8,128)(2,1)S(1)} %get-tuple-element.64.refs_8_), channel_id=1, source_target_pairs={{0,16},{8,24},{16,0},{24,8},{1,17},{9,25},{17,1},{25,9},{2,18},{10... | collective-permute-start | bytes 786440 | tf_op jit(solution)/shard_map/ppermute | solution.py:271
  28.7 10.3 %collective-permute-start.17 = (bf16[896,256]{1,0:T(8,128)(2,1)S(1)}, bf16[896,256]{1,0:T(8,128)(2,1)S(1)}, u32[]{:S(2)}, u32[]{:S(2)}) collective-permute-start(bf16[896,256]{1,0:T(8,128)(2,1)S(1)} %get-tuple-element.74.refs_0_), channel_id=1, source_target_pairs={{0,8},{8,0},{16,24},{24,16},{1,9},{9,1},{17,25},{25,17},{2,10},{10... | collective-permute-start | bytes 1376264 | tf_op jit(solution)/shard_map/ppermute | solution.py:271
  28.8 2.0 %collective-permute-start.14 = (bf16[2,4,2,16,256]{4,3,2,1,0:T(8,128)(2,1)S(1)}, bf16[2,4,2,16,256]{4,3,2,1,0:T(8,128)(2,1)S(1)}, u32[]{:S(2)}, u32[]{:S(2)}) collective-permute-start(bf16[2,4,2,16,256]{4,3,2,1,0:T(8,128)(2,1)S(1)} %get-tuple-element.68), channel_id=1, source_target_pairs={{0,8},{8,0},{16,24},{24,16},{1,9},{9,1},{17,25},{25,17},{2,10},{10... | collective-permute-start | bytes 393224 | tf_op jit(solution)/shard_map/ppermute | solution.py:271
  29.3 7.6 %collective-permute-start.16 = (bf16[384,256]{1,0:T(8,128)(2,1)S(1)}, bf16[384,256]{1,0:T(8,128)(2,1)S(1)}, u32[]{:S(2)}, u32[]{:S(2)}) collective-permute-start(bf16[384,256]{1,0:T(8,128)(2,1)S(1)} %get-tuple-element.66.refs_9_), channel_id=1, source_target_pairs={{0,16},{8,24},{16,0},{24,8},{1,17},{9,25},{17,1},{25,9},{2,18},{10... | collective-permute-start | bytes 589832 | tf_op jit(solution)/shard_map/ppermute | solution.py:271
  30.8 6.8 %collective-permute-start.15 = (bf16[1,4,2,16,256]{4,3,2,1,0:T(8,128)(2,1)S(1)}, bf16[1,4,2,16,256]{4,3,2,1,0:T(8,128)(2,1)S(1)}, u32[]{:S(2)}, u32[]{:S(2)}) collective-permute-start(bf16[1,4,2,16,256]{4,3,2,1,0:T(8,128)(2,1)S(1)} %get-tuple-element.71), channel_id=1, source_target_pairs={{0,16},{8,24},{16,0},{24,8},{1,17},{9,25},{17,1},{25,9},{2,18},{10... | collective-permute-start | bytes 196616 | tf_op jit(solution)/shard_map/ppermute | solution.py:271
  32.1 6.9 %collective-permute-start.18 = (bf16[512,256]{1,0:T(8,128)(2,1)S(1)}, bf16[512,256]{1,0:T(8,128)(2,1)S(1)}, u32[]{:S(2)}, u32[]{:S(2)}) collective-permute-start(bf16[512,256]{1,0:T(8,128)(2,1)S(1)} %collective-permute-done.10.refs_1_), channel_id=1, source_target_pairs={{0,8},{8,0},{16,24},{24,16},{1,9},{9,1},{17,25},{25,17},{2,10},{10... | collective-permute-start | bytes 786440 | tf_op jit(solution)/shard_map/ppermute | solution.py:271
  33.7 3.9 %copy-start = (bf16[1,128,256]{2,1,0:T(8,128)(2,1)S(1)}, bf16[1,128,256]{2,1,0:T(8,128)(2,1)}, u32[]{:S(2)}) copy-start(bf16[1,128,256]{2,1,0:T(8,128)(2,1)} %gate.1) | copy-start | bytes 196612
  33.7 3.9 %copy-start.1 = (bf16[1,128,256]{2,1,0:T(8,128)(2,1)S(1)}, bf16[1,128,256]{2,1,0:T(8,128)(2,1)}, u32[]{:S(2)}) copy-start(bf16[1,128,256]{2,1,0:T(8,128)(2,1)} %up.1) | copy-start | bytes 196612
  37.6 1.4 %collective-permute-start.19 = (bf16[384,256]{1,0:T(8,128)(2,1)S(1)}, bf16[384,256]{1,0:T(8,128)(2,1)S(1)}, u32[]{:S(2)}, u32[]{:S(2)}) collective-permute-start(bf16[384,256]{1,0:T(8,128)(2,1)S(1)} %collective-permute-done.16.refs_2_), channel_id=1, source_target_pairs={{0,8},{8,0},{16,24},{24,16},{1,9},{9,1},{17,25},{25,17},{2,10},{10... | collective-permute-start | bytes 589832 | tf_op jit(solution)/shard_map/ppermute | solution.py:271

commit v2 on v0

--- a/solution.py
+++ b/solution.py
@@ -315,7 +315,7 @@
         cost_estimate=cost(0, high * across * 24),
         name="fetch",
     )(hidden, pinned(master_weight), pinned(first_moment), pinned(second_moment))
-    order = [*range(pieces // 2, len(offsets)), *range(1, pieces // 2), 0]
+    order = [*range(len(offsets) - 1, pieces // 2 - 1, -1), *range(1, pieces // 2), 0]
     turned, state = lax.optimization_barrier(([blocks[n] for n in order], state))
     blocks = [turned[order.index(n)] for n in range(len(offsets))]
     other = pl.pallas_call(

time: 40.2 us -> 40.1 us (level)
  starting transfers between devices: 18.9 us -> 16.9 us
  waiting for transfers between devices: 11.4 us -> 13.3 us
    ppermute x11, starting transfers between devices: 6.26 us -> 4.2 us  [over_dp(): return lax.ppermute(x, 'dp', [(i, i ^ d) for i in range(pieces)])]
    ppermute x11, waiting for transfers between devices: 4.71 us -> 6.36 us  [over_dp(): return lax.ppermute(x, 'dp', [(i, i ^ d) for i in range(pieces)])]
  transfers between devices with their start and end apart: 20 -> 20, of which waited for: 10 -> 12; matrix products, arithmetic and copies ran while one was open for 0% -> 0% of each run, Pallas kernels for 17% -> 17%
where the time goes in v2:
time: 40.1 us; the launch traced here: 40 us
  starting transfers between devices  16.9 us (42%)
  waiting for transfers between devices  13.3 us (33%)
  Pallas kernels  8.93 us (22%)
  between operations  0.76 us (2%)
    ppermute x6, starting transfers between devices, local(): lax.ppermute(piece, 'expert', [(k, k ^ d) for k in range(sources)])  7.04 us
    ppermute x11, waiting for transfers between devices, over_dp(): return lax.ppermute(x, 'dp', [(i, i ^ d) for i in range(pieces)])  6.36 us
    ppermute x3, starting transfers between devices, local(): blocks[n] = lax.ppermute(blocks[n], ('dp', 'expert'), pairs)  5.67 us
    ppermute x11, starting transfers between devices, over_dp(): return lax.ppermute(x, 'dp', [(i, i ^ d) for i in range(pieces)])  4.2 us
    ppermute x6, waiting for transfers between devices, local(): lax.ppermute(piece, 'expert', [(k, k ^ d) for k in range(sources)])  3.95 us
    ppermute x3, waiting for transfers between devices, local(): blocks[n] = lax.ppermute(blocks[n], ('dp', 'expert'), pairs)  3.03 us
    pallas_call x2, Pallas kernels, join(): pl.pallas_call(functools.partial(join_kernel, high, [entry[:3] for entry...  1.9 us
    pallas_call x1, Pallas kernels, local(): pl.pallas_call(fetch_kernel, out_shape=[shape((high, across), f32)] * 3,...  1.76 us
  transfers between devices with their start and end apart: 20, of which 12 were waited for; matrix products, arithmetic and copies ran while one was open for 0% of the time, Pallas kernels for 17%

profile of v2, /device:TPU:0, one launch (start us, length us, event | category | flops | bytes accessed | tf_op | source)
XLA Modules:
  0.0 40.0 jit_solution(4342957911901251544)
XLA Ops:
  0.6 1.2 %scale.1 = (bf16[4,2,16,256]{3,2,1,0:T(8,128)(2,1)S(1)}, bf16[2,16,896]{2,1,0:T(8,128)(2,1)S(1)}, bf16[2,16,896]{2,1,0:T(8,128)(2,1)S(1)}, bf16[2,16,896]{2,1,0:T(8,128)(2,1)S(1)}, bf16[2,16,896]{2,1,0:T(8,128)(2,1)S(1)}) custom-call(s32[1,2]{1,0:T(1,128)} %counts_in.1, f32[1,2,16]{2,1,0:T(2,128)} %router_in.1, bf16[1,2,16,3584]{3,2,1,0:T(8,128)(2,1)} %rows_in.1, ...), custom_call_target="tpu_custom_call" | custom-call | tf_op jit(solution)/shard_map/scale/pallas_call | solution.py:275
  1.9 5.0 %collective-permute-start = (bf16[2,16,896]{2,1,0:T(8,128)(2,1)S(1)}, bf16[2,16,896]{2,1,0:T(8,128)(2,1)S(1)}, u32[]{:S(2)}, u32[]{:S(2)}) collective-permute-start(bf16[2,16,896]{2,1,0:T(8,128)(2,1)S(1)} %get-tuple-element.48), channel_id=1, source_target_pairs={{0,20},{1,21},{2,22},{3,23},{4,16},{5,17},{6,18},{7,19},{8,28},{9,... | collective-permute-start | bytes 172040 | tf_op jit(solution)/shard_map/ppermute | solution.py:307
  6.9 0.3 collective-permute-start.1
  7.2 0.3 collective-permute-start.2
  7.5 1.8 %fetch.1 = (f32[896,256]{1,0:T(8,128)S(1)}, f32[896,256]{1,0:T(8,128)S(1)}, f32[896,256]{1,0:T(8,128)S(1)}) custom-call(bf16[4,2,16,256]{3,2,1,0:T(8,128)(2,1)S(1)} %get-tuple-element.52.after.refs_0_, f32[896,256]{1,0:T(8,128)} %refs_0_.1, f32[896,256]{1,0:T(8,128)} %refs_1_.1, f32[896,256]{1,0:T(8,128)} %refs_2_.1), custom_call_target="tpu_custom_call" | custom-call | bytes 5505024 | tf_op jit(solution)/shard_map/fetch/pallas_call | solution.py:308
  9.3 0.5 %collective-permute-done.refs_0_.refs_3_ = bf16[2,16,896]{2,1,0:T(8,128)(2,1)S(1)} collective-permute-done((bf16[2,16,896]{2,1,0:T(8,128)(2,1)S(1)}, bf16[2,16,896]{2,1,0:T(8,128)(2,1)S(1)}, u32[]{:S(2)}, u32[]{:S(2)}) %collective-permute-start) | collective-permute-done | bytes 57376 | tf_op jit(solution)/shard_map/ppermute | solution.py:307
  9.8 2.6 %collective-permute-done.1.refs_1_.refs_2_ = bf16[2,16,896]{2,1,0:T(8,128)(2,1)S(1)} collective-permute-done((bf16[2,16,896]{2,1,0:T(8,128)(2,1)S(1)}, bf16[2,16,896]{2,1,0:T(8,128)(2,1)S(1)}, u32[]{:S(2)}, u32[]{:S(2)}) %collective-permute-start.1) | collective-permute-done | bytes 57376 | tf_op jit(solution)/shard_map/ppermute | solution.py:307
  12.3 0.0 collective-permute-done.2.refs_2_.refs_1_
  12.3 0.1 collective-permute-start.3
  12.4 0.5 %collective-permute-start.8 = (bf16[4,2,16,256]{3,2,1,0:T(8,128)(2,1)S(1)}, bf16[4,2,16,256]{3,2,1,0:T(8,128)(2,1)S(1)}, u32[]{:S(2)}, u32[]{:S(2)}) collective-permute-start(bf16[4,2,16,256]{3,2,1,0:T(8,128)(2,1)S(1)} %get-tuple-element.52.after.refs_0_), channel_id=1, source_target_pairs={{0,16},{8,24},{16,0},{24,8},{1,17},{9,25},{17,1},{25,9},{2,18},{10... | collective-permute-start | bytes 196616 | tf_op jit(solution)/shard_map/ppermute | solution.py:269
  12.9 0.8 %collective-permute-done.3.other = bf16[4,16,896]{2,1,0:T(8,128)(2,1)S(1)} collective-permute-done((bf16[4,16,896]{2,1,0:T(8,128)(2,1)S(1)}, bf16[4,16,896]{2,1,0:T(8,128)(2,1)S(1)}, u32[]{:S(2)}, u32[]{:S(2)}) %collective-permute-start.3) | collective-permute-done | bytes 114720 | tf_op jit(solution)/shard_map/ppermute | solution.py:269
  13.8 1.6 %collective-permute-start.6 = (bf16[8,16,512]{2,1,0:T(8,128)(2,1)S(1)}, bf16[8,16,512]{2,1,0:T(8,128)(2,1)S(1)}, u32[]{:S(2)}, u32[]{:S(2)}) collective-permute-start(bf16[8,16,512]{2,1,0:T(8,128)(2,1)S(1)} %get-tuple-element.60.refs_0_), channel_id=1, source_target_pairs={{0,1},{1,0},{2,3},{3,2},{4,5},{5,4},{6,7},{7,6},{8,9},{9,8},{10,11... | collective-permute-start | bytes 393224 | tf_op jit(solution)/shard_map/ppermute | solution.py:360
  15.3 1.2 %collective-permute-start.5 = (bf16[8,16,512]{2,1,0:T(8,128)(2,1)S(1)}, bf16[8,16,512]{2,1,0:T(8,128)(2,1)S(1)}, u32[]{:S(2)}, u32[]{:S(2)}) collective-permute-start(bf16[8,16,512]{2,1,0:T(8,128)(2,1)S(1)} %get-tuple-element.60.refs_0_), channel_id=1, source_target_pairs={{0,2},{1,3},{2,0},{3,1},{4,6},{5,7},{6,4},{7,5},{8,10},{9,11},{10,... | collective-permute-start | bytes 393224 | tf_op jit(solution)/shard_map/ppermute | solution.py:360
  16.6 0.8 %collective-permute-start.4 = (bf16[8,16,512]{2,1,0:T(8,128)(2,1)S(1)}, bf16[8,16,512]{2,1,0:T(8,128)(2,1)S(1)}, u32[]{:S(2)}, u32[]{:S(2)}) collective-permute-start(bf16[8,16,512]{2,1,0:T(8,128)(2,1)S(1)} %get-tuple-element.60.refs_0_), channel_id=1, source_target_pairs={{0,3},{1,2},{2,1},{3,0},{4,7},{5,6},{6,5},{7,4},{8,11},{9,10},{10,... | collective-permute-start | bytes 393224 | tf_op jit(solution)/shard_map/ppermute | solution.py:360
  17.3 0.0 collective-permute-start.7
  17.3 0.0 collective-permute-done.8.refs_2_
  17.3 0.5 %collective-permute-start.9 = (bf16[4,2,16,256]{3,2,1,0:T(8,128)(2,1)S(1)}, bf16[4,2,16,256]{3,2,1,0:T(8,128)(2,1)S(1)}, u32[]{:S(2)}, u32[]{:S(2)}) collective-permute-start(bf16[4,2,16,256]{3,2,1,0:T(8,128)(2,1)S(1)} %collective-permute-done.8.refs_2_), channel_id=1, source_target_pairs={{0,8},{8,0},{16,24},{24,16},{1,9},{9,1},{17,25},{25,17},{2,10},{10... | collective-permute-start | bytes 196616 | tf_op jit(solution)/shard_map/ppermute | solution.py:269
  17.8 0.7 %collective-permute-done.7.refs_1_ = bf16[4,2,16,256]{3,2,1,0:T(8,128)(2,1)S(1)} collective-permute-done((bf16[4,2,16,256]{3,2,1,0:T(8,128)(2,1)S(1)}, bf16[4,2,16,256]{3,2,1,0:T(8,128)(2,1)S(1)}, u32[]{:S(2)}, u32[]{:S(2)}) %collective-permute-start.7) | collective-permute-done | bytes 65568 | tf_op jit(solution)/shard_map/ppermute | solution.py:269
  18.6 1.5 %collective-permute-start.13 = (bf16[8,16,384]{2,1,0:T(8,128)(2,1)S(1)}, bf16[8,16,384]{2,1,0:T(8,128)(2,1)S(1)}, u32[]{:S(2)}, u32[]{:S(2)}) collective-permute-start(bf16[8,16,384]{2,1,0:T(8,128)(2,1)S(1)} %get-tuple-element.65.refs_0_.refs_4_), channel_id=1, source_target_pairs={{0,1},{1,0},{2,3},{3,2},{4,5},{5,4},{6,7},{7,6},{8,9},{9,8},{10,11... | collective-permute-start | bytes 294920 | tf_op jit(solution)/shard_map/ppermute | solution.py:360
  20.1 0.0 collective-permute-done.9.refs_3_
  20.1 1.2 %collective-permute-start.12 = (bf16[8,16,384]{2,1,0:T(8,128)(2,1)S(1)}, bf16[8,16,384]{2,1,0:T(8,128)(2,1)S(1)}, u32[]{:S(2)}, u32[]{:S(2)}) collective-permute-start(bf16[8,16,384]{2,1,0:T(8,128)(2,1)S(1)} %get-tuple-element.65.refs_0_.refs_4_), channel_id=1, source_target_pairs={{0,2},{1,3},{2,0},{3,1},{4,6},{5,7},{6,4},{7,5},{8,10},{9,11},{10,... | collective-permute-start | bytes 294920 | tf_op jit(solution)/shard_map/ppermute | solution.py:360
  21.3 0.0 collective-permute-done.6.refs_3_
  21.3 0.8 %collective-permute-start.11 = (bf16[8,16,384]{2,1,0:T(8,128)(2,1)S(1)}, bf16[8,16,384]{2,1,0:T(8,128)(2,1)S(1)}, u32[]{:S(2)}, u32[]{:S(2)}) collective-permute-start(bf16[8,16,384]{2,1,0:T(8,128)(2,1)S(1)} %get-tuple-element.65.refs_0_.refs_4_), channel_id=1, source_target_pairs={{0,3},{1,2},{2,1},{3,0},{4,7},{5,6},{6,5},{7,4},{8,11},{9,10},{10,... | collective-permute-start | bytes 294920 | tf_op jit(solution)/shard_map/ppermute | solution.py:360
  22.1 0.0 collective-permute-done.5.refs_2_
  22.1 2.0 %collective-permute-done.4.refs_1_ = bf16[8,16,512]{2,1,0:T(8,128)(2,1)S(1)} collective-permute-done((bf16[8,16,512]{2,1,0:T(8,128)(2,1)S(1)}, bf16[8,16,512]{2,1,0:T(8,128)(2,1)S(1)}, u32[]{:S(2)}, u32[]{:S(2)}) %collective-permute-start.4) | collective-permute-done | bytes 131104 | tf_op jit(solution)/shard_map/ppermute | solution.py:360
  24.1 0.7 %update.2 = (bf16[512,256]{1,0:T(8,128)(2,1)S(1)}, f32[512,256]{1,0:T(8,128)S(1)}, f32[512,256]{1,0:T(8,128)S(1)}, f32[512,256]{1,0:T(8,128)S(1)}) custom-call(bf16[8,16,512]{2,1,0:T(8,128)(2,1)S(1)} %get-tuple-element.60.refs_0_, bf16[8,16,512]{2,1,0:T(8,128)(2,1)S(1)} %collective-permute-done.4.refs_1_, ...), custom_call_target="tpu_custom_call" | custom-call | flops 134217728 | bytes 5963776 | tf_op jit(solution)/shard_map/update/pallas_call | solution.py:367
  24.8 0.9 %collective-permute-start.10 = (bf16[512,256]{1,0:T(8,128)(2,1)S(1)}, bf16[512,256]{1,0:T(8,128)(2,1)S(1)}, u32[]{:S(2)}, u32[]{:S(2)}) collective-permute-start(bf16[512,256]{1,0:T(8,128)(2,1)S(1)} %get-tuple-element.64.refs_8_), channel_id=1, source_target_pairs={{0,16},{8,24},{16,0},{24,8},{1,17},{9,25},{17,1},{25,9},{2,18},{10... | collective-permute-start | bytes 786440 | tf_op jit(solution)/shard_map/ppermute | solution.py:269
  25.7 0.3 collective-permute-done.13.refs_3_.refs_7_
  25.9 0.4 collective-permute-done.12.refs_2_.refs_6_
  26.3 1.3 %collective-permute-done.11.refs_1_.refs_5_ = bf16[8,16,384]{2,1,0:T(8,128)(2,1)S(1)} collective-permute-done((bf16[8,16,384]{2,1,0:T(8,128)(2,1)S(1)}, bf16[8,16,384]{2,1,0:T(8,128)(2,1)S(1)}, u32[]{:S(2)}, u32[]{:S(2)}) %collective-permute-start.11) | collective-permute-done | bytes 98336 | tf_op jit(solution)/shard_map/ppermute | solution.py:360
  27.6 0.6 %update.3 = (bf16[384,256]{1,0:T(8,128)(2,1)S(1)}, f32[384,256]{1,0:T(8,128)S(1)}, f32[384,256]{1,0:T(8,128)S(1)}, f32[384,256]{1,0:T(8,128)S(1)}) custom-call(bf16[8,16,384]{2,1,0:T(8,128)(2,1)S(1)} %get-tuple-element.65.refs_0_.refs_4_, bf16[8,16,384]{2,1,0:T(8,128)(2,1)S(1)} %collective-permute-done.11.refs_1_.refs_5_, ...), custom_call_target="tpu_custom_call" | custom-call | flops 100663296 | bytes 5963776 | tf_op jit(solution)/shard_map/update/pallas_call | solution.py:367
  28.2 0.4 %partial.1 = (f32[2,4,2,16,256]{4,3,2,1,0:T(8,128)S(1)}, bf16[2,4,2,16,256]{4,3,2,1,0:T(8,128)(2,1)S(1)}, bf16[896,256]{1,0:T(8,128)(2,1)S(1)}) custom-call(bf16[8,16,512]{2,1,0:T(8,128)(2,1)S(1)} %get-tuple-element.60.refs_0_, bf16[8,16,512]{2,1,0:T(8,128)(2,1)S(1)} %collective-permute-done.4.refs_1_, ...), custom_call_target="tpu_custom_call" | custom-call | flops 234881024 | bytes 2752512 | tf_op jit(solution)/shard_map/partial/pallas_call | solution.py:385
  28.6 0.1 collective-permute-start.17
  28.7 0.5 %collective-permute-start.14 = (bf16[2,4,2,16,256]{4,3,2,1,0:T(8,128)(2,1)S(1)}, bf16[2,4,2,16,256]{4,3,2,1,0:T(8,128)(2,1)S(1)}, u32[]{:S(2)}, u32[]{:S(2)}) collective-permute-start(bf16[2,4,2,16,256]{4,3,2,1,0:T(8,128)(2,1)S(1)} %get-tuple-element.68), channel_id=1, source_target_pairs={{0,8},{8,0},{16,24},{24,16},{1,9},{9,1},{17,25},{25,17},{2,10},{10... | collective-permute-start | bytes 393224 | tf_op jit(solution)/shard_map/ppermute | solution.py:269
  29.2 0.8 %collective-permute-start.16 = (bf16[384,256]{1,0:T(8,128)(2,1)S(1)}, bf16[384,256]{1,0:T(8,128)(2,1)S(1)}, u32[]{:S(2)}, u32[]{:S(2)}) collective-permute-start(bf16[384,256]{1,0:T(8,128)(2,1)S(1)} %get-tuple-element.66.refs_9_), channel_id=1, source_target_pairs={{0,16},{8,24},{16,0},{24,8},{1,17},{9,25},{17,1},{25,9},{2,18},{10... | collective-permute-start | bytes 589832 | tf_op jit(solution)/shard_map/ppermute | solution.py:269
  30.0 0.7 %collective-permute-done.14.arrived = bf16[2,4,2,16,256]{4,3,2,1,0:T(8,128)(2,1)S(1)} collective-permute-done((bf16[2,4,2,16,256]{4,3,2,1,0:T(8,128)(2,1)S(1)}, bf16[2,4,2,16,256]{4,3,2,1,0:T(8,128)(2,1)S(1)}, u32[]{:S(2)}, u32[]{:S(2)}) %collective-permute-start.14) | collective-permute-done | bytes 131104 | tf_op jit(solution)/shard_map/ppermute | solution.py:269
  30.7 0.9 %collective-permute-start.15 = (bf16[1,4,2,16,256]{4,3,2,1,0:T(8,128)(2,1)S(1)}, bf16[1,4,2,16,256]{4,3,2,1,0:T(8,128)(2,1)S(1)}, u32[]{:S(2)}, u32[]{:S(2)}) collective-permute-start(bf16[1,4,2,16,256]{4,3,2,1,0:T(8,128)(2,1)S(1)} %get-tuple-element.71), channel_id=1, source_target_pairs={{0,16},{8,24},{16,0},{24,8},{1,17},{9,25},{17,1},{25,9},{2,18},{10... | collective-permute-start | bytes 196616 | tf_op jit(solution)/shard_map/ppermute | solution.py:269
  31.6 0.0 collective-permute-done.10.refs_1_
  31.6 0.0 collective-permute-start.18
  31.6 1.6 %store.1 = (f32[896,256]{1,0:T(8,128)}, f32[896,256]{1,0:T(8,128)}, f32[896,256]{1,0:T(8,128)}) custom-call(f32[512,256]{1,0:T(8,128)S(1)} %get-tuple-element.76.refs_0_, f32[512,256]{1,0:T(8,128)S(1)} %get-tuple-element.77.refs_1_, f32[512,256]{1,0:T(8,128)S(1)} %get-tuple-element.78.refs_2_, f32[384,256]{1,0:T(8,128)S(1)} %get-tuple-element.79.refs_3_, ...), custom_call_target="tpu_custom_call" | custom-call | bytes 5505024 | tf_op jit(solution)/shard_map/store/pallas_call | solution.py:428
  33.2 0.0 copy-start
  33.2 0.0 copy-start.1
  33.2 0.9 %join.2.refs_4_ = bf16[3584,256]{1,0:T(8,128)(2,1)} custom-call(bf16[896,256]{1,0:T(8,128)(2,1)S(1)} %get-tuple-element.74.refs_0_, bf16[512,256]{1,0:T(8,128)(2,1)S(1)} %collective-permute-done.10.refs_1_), custom_call_target="tpu_custom_call" | custom-call | tf_op jit(solution)/shard_map/join/pallas_call | solution.py:440
  34.1 2.7 %collective-permute-done.16.refs_2_ = bf16[384,256]{1,0:T(8,128)(2,1)S(1)} collective-permute-done((bf16[384,256]{1,0:T(8,128)(2,1)S(1)}, bf16[384,256]{1,0:T(8,128)(2,1)S(1)}, u32[]{:S(2)}, u32[]{:S(2)}) %collective-permute-start.16) | collective-permute-done | bytes 196640 | tf_op jit(solution)/shard_map/ppermute | solution.py:269
  36.8 0.7 %collective-permute-done.15.arrived = bf16[1,4,2,16,256]{4,3,2,1,0:T(8,128)(2,1)S(1)} collective-permute-done((bf16[1,4,2,16,256]{4,3,2,1,0:T(8,128)(2,1)S(1)}, bf16[1,4,2,16,256]{4,3,2,1,0:T(8,128)(2,1)S(1)}, u32[]{:S(2)}, u32[]{:S(2)}) %collective-permute-start.15) | collective-permute-done | bytes 65568 | tf_op jit(solution)/shard_map/ppermute | solution.py:269
  37.5 0.0 collective-permute-start.19
  37.5 0.0 copy-done
  37.5 0.0 copy-done.1
  37.5 0.7 %gates.1 = (bf16[1,128,256]{2,1,0:T(8,128)(2,1)}, bf16[1,128,256]{2,1,0:T(8,128)(2,1)}) custom-call(bf16[1,128,256]{2,1,0:T(8,128)(2,1)S(1)} %copy-done, bf16[1,128,256]{2,1,0:T(8,128)(2,1)S(1)} %copy-done.1, f32[1,4,2,16,256]{4,3,2,1,0:T(8,128)S(1)} %get-tuple-element.70.held, bf16[1,4,2,16,256]{4,3,2,1,0:T(8,128)(2,1)S(1)} %collective-permute-done.15.arrived), custom_call_target="tpu_custom_call" | custom-call | tf_op jit(solution)/shard_map/gates/pallas_call | solution.py:419
  38.2 0.7 %collective-permute-done.19.refs_3_ = bf16[384,256]{1,0:T(8,128)(2,1)S(1)} collective-permute-done((bf16[384,256]{1,0:T(8,128)(2,1)S(1)}, bf16[384,256]{1,0:T(8,128)(2,1)S(1)}, u32[]{:S(2)}, u32[]{:S(2)}) %collective-permute-start.19) | collective-permute-done | bytes 196640 | tf_op jit(solution)/shard_map/ppermute | solution.py:269
  38.9 0.0 collective-permute-done.17.refs_0_
  38.9 0.0 collective-permute-done.18.refs_1_
  38.9 1.0 %join.3 = bf16[3584,256]{1,0:T(8,128)(2,1)} custom-call(bf16[896,256]{1,0:T(8,128)(2,1)S(1)} %collective-permute-done.17.refs_0_, bf16[512,256]{1,0:T(8,128)(2,1)S(1)} %collective-permute-done.18.refs_1_, bf16[384,256]{1,0:T(8,128)(2,1)S(1)} %collective-permute-done.16.refs_2_, ...), custom_call_target="tpu_custom_call", output_to_operand_aliasing={{}: (4, {})} | custom-call | tf_op jit(solution)/shard_map/join/pallas_call | solution.py:440
  (4 shorter events, 0.1 us)
Async XLA Ops:
  1.9 7.9 %collective-permute-start = (bf16[2,16,896]{2,1,0:T(8,128)(2,1)S(1)}, bf16[2,16,896]{2,1,0:T(8,128)(2,1)S(1)}, u32[]{:S(2)}, u32[]{:S(2)}) collective-permute-start(bf16[2,16,896]{2,1,0:T(8,128)(2,1)S(1)} %get-tuple-element.48), channel_id=1, source_target_pairs={{0,20},{1,21},{2,22},{3,23},{4,16},{5,17},{6,18},{7,19},{8,28},{9,... | collective-permute-start | bytes 172040 | tf_op jit(solution)/shard_map/ppermute | solution.py:307
  6.9 5.4 %collective-permute-start.1 = (bf16[2,16,896]{2,1,0:T(8,128)(2,1)S(1)}, bf16[2,16,896]{2,1,0:T(8,128)(2,1)S(1)}, u32[]{:S(2)}, u32[]{:S(2)}) collective-permute-start(bf16[2,16,896]{2,1,0:T(8,128)(2,1)S(1)} %get-tuple-element.49), channel_id=1, source_target_pairs={{0,4},{1,5},{2,6},{3,7},{4,0},{5,1},{6,2},{7,3},{8,12},{9,13},{10,... | collective-permute-start | bytes 172040 | tf_op jit(solution)/shard_map/ppermute | solution.py:307
  7.2 5.1 %collective-permute-start.2 = (bf16[2,16,896]{2,1,0:T(8,128)(2,1)S(1)}, bf16[2,16,896]{2,1,0:T(8,128)(2,1)S(1)}, u32[]{:S(2)}, u32[]{:S(2)}) collective-permute-start(bf16[2,16,896]{2,1,0:T(8,128)(2,1)S(1)} %get-tuple-element.50), channel_id=1, source_target_pairs={{0,16},{1,17},{2,18},{3,19},{4,20},{5,21},{6,22},{7,23},{8,24},{9,... | collective-permute-start | bytes 172040 | tf_op jit(solution)/shard_map/ppermute | solution.py:307
  12.3 1.4 %collective-permute-start.3 = (bf16[4,16,896]{2,1,0:T(8,128)(2,1)S(1)}, bf16[4,16,896]{2,1,0:T(8,128)(2,1)S(1)}, u32[]{:S(2)}, u32[]{:S(2)}) collective-permute-start(bf16[4,16,896]{2,1,0:T(8,128)(2,1)S(1)} %share.1), channel_id=1, source_target_pairs={{0,8},{8,0},{16,24},{24,16},{1,9},{9,1},{17,25},{25,17},{2,10},{10... | collective-permute-start | bytes 344072 | tf_op jit(solution)/shard_map/ppermute | solution.py:269
  12.4 4.9 %collective-permute-start.8 = (bf16[4,2,16,256]{3,2,1,0:T(8,128)(2,1)S(1)}, bf16[4,2,16,256]{3,2,1,0:T(8,128)(2,1)S(1)}, u32[]{:S(2)}, u32[]{:S(2)}) collective-permute-start(bf16[4,2,16,256]{3,2,1,0:T(8,128)(2,1)S(1)} %get-tuple-element.52.after.refs_0_), channel_id=1, source_target_pairs={{0,16},{8,24},{16,0},{24,8},{1,17},{9,25},{17,1},{25,9},{2,18},{10... | collective-permute-start | bytes 196616 | tf_op jit(solution)/shard_map/ppermute | solution.py:269
  13.8 7.6 %collective-permute-start.6 = (bf16[8,16,512]{2,1,0:T(8,128)(2,1)S(1)}, bf16[8,16,512]{2,1,0:T(8,128)(2,1)S(1)}, u32[]{:S(2)}, u32[]{:S(2)}) collective-permute-start(bf16[8,16,512]{2,1,0:T(8,128)(2,1)S(1)} %get-tuple-element.60.refs_0_), channel_id=1, source_target_pairs={{0,1},{1,0},{2,3},{3,2},{4,5},{5,4},{6,7},{7,6},{8,9},{9,8},{10,11... | collective-permute-start | bytes 393224 | tf_op jit(solution)/shard_map/ppermute | solution.py:360
  15.3 6.7 %collective-permute-start.5 = (bf16[8,16,512]{2,1,0:T(8,128)(2,1)S(1)}, bf16[8,16,512]{2,1,0:T(8,128)(2,1)S(1)}, u32[]{:S(2)}, u32[]{:S(2)}) collective-permute-start(bf16[8,16,512]{2,1,0:T(8,128)(2,1)S(1)} %get-tuple-element.60.refs_0_), channel_id=1, source_target_pairs={{0,2},{1,3},{2,0},{3,1},{4,6},{5,7},{6,4},{7,5},{8,10},{9,11},{10,... | collective-permute-start | bytes 393224 | tf_op jit(solution)/shard_map/ppermute | solution.py:360
  16.6 7.6 %collective-permute-start.4 = (bf16[8,16,512]{2,1,0:T(8,128)(2,1)S(1)}, bf16[8,16,512]{2,1,0:T(8,128)(2,1)S(1)}, u32[]{:S(2)}, u32[]{:S(2)}) collective-permute-start(bf16[8,16,512]{2,1,0:T(8,128)(2,1)S(1)} %get-tuple-element.60.refs_0_), channel_id=1, source_target_pairs={{0,3},{1,2},{2,1},{3,0},{4,7},{5,6},{6,5},{7,4},{8,11},{9,10},{10,... | collective-permute-start | bytes 393224 | tf_op jit(solution)/shard_map/ppermute | solution.py:360
  17.3 1.3 %collective-permute-start.7 = (bf16[4,2,16,256]{3,2,1,0:T(8,128)(2,1)S(1)}, bf16[4,2,16,256]{3,2,1,0:T(8,128)(2,1)S(1)}, u32[]{:S(2)}, u32[]{:S(2)}) collective-permute-start(bf16[4,2,16,256]{3,2,1,0:T(8,128)(2,1)S(1)} %get-tuple-element.52.after.refs_0_), channel_id=1, source_target_pairs={{0,8},{8,0},{16,24},{24,16},{1,9},{9,1},{17,25},{25,17},{2,10},{10... | collective-permute-start | bytes 196616 | tf_op jit(solution)/shard_map/ppermute | solution.py:269
  17.3 2.8 %collective-permute-start.9 = (bf16[4,2,16,256]{3,2,1,0:T(8,128)(2,1)S(1)}, bf16[4,2,16,256]{3,2,1,0:T(8,128)(2,1)S(1)}, u32[]{:S(2)}, u32[]{:S(2)}) collective-permute-start(bf16[4,2,16,256]{3,2,1,0:T(8,128)(2,1)S(1)} %collective-permute-done.8.refs_2_), channel_id=1, source_target_pairs={{0,8},{8,0},{16,24},{24,16},{1,9},{9,1},{17,25},{25,17},{2,10},{10... | collective-permute-start | bytes 196616 | tf_op jit(solution)/shard_map/ppermute | solution.py:269
  18.6 7.4 %collective-permute-start.13 = (bf16[8,16,384]{2,1,0:T(8,128)(2,1)S(1)}, bf16[8,16,384]{2,1,0:T(8,128)(2,1)S(1)}, u32[]{:S(2)}, u32[]{:S(2)}) collective-permute-start(bf16[8,16,384]{2,1,0:T(8,128)(2,1)S(1)} %get-tuple-element.65.refs_0_.refs_4_), channel_id=1, source_target_pairs={{0,1},{1,0},{2,3},{3,2},{4,5},{5,4},{6,7},{7,6},{8,9},{9,8},{10,11... | collective-permute-start | bytes 294920 | tf_op jit(solution)/shard_map/ppermute | solution.py:360
  20.1 6.2 %collective-permute-start.12 = (bf16[8,16,384]{2,1,0:T(8,128)(2,1)S(1)}, bf16[8,16,384]{2,1,0:T(8,128)(2,1)S(1)}, u32[]{:S(2)}, u32[]{:S(2)}) collective-permute-start(bf16[8,16,384]{2,1,0:T(8,128)(2,1)S(1)} %get-tuple-element.65.refs_0_.refs_4_), channel_id=1, source_target_pairs={{0,2},{1,3},{2,0},{3,1},{4,6},{5,7},{6,4},{7,5},{8,10},{9,11},{10,... | collective-permute-start | bytes 294920 | tf_op jit(solution)/shard_map/ppermute | solution.py:360
  21.3 6.3 %collective-permute-start.11 = (bf16[8,16,384]{2,1,0:T(8,128)(2,1)S(1)}, bf16[8,16,384]{2,1,0:T(8,128)(2,1)S(1)}, u32[]{:S(2)}, u32[]{:S(2)}) collective-permute-start(bf16[8,16,384]{2,1,0:T(8,128)(2,1)S(1)} %get-tuple-element.65.refs_0_.refs_4_), channel_id=1, source_target_pairs={{0,3},{1,2},{2,1},{3,0},{4,7},{5,6},{6,5},{7,4},{8,11},{9,10},{10,... | collective-permute-start | bytes 294920 | tf_op jit(solution)/shard_map/ppermute | solution.py:360
  24.8 6.8 %collective-permute-start.10 = (bf16[512,256]{1,0:T(8,128)(2,1)S(1)}, bf16[512,256]{1,0:T(8,128)(2,1)S(1)}, u32[]{:S(2)}, u32[]{:S(2)}) collective-permute-start(bf16[512,256]{1,0:T(8,128)(2,1)S(1)} %get-tuple-element.64.refs_8_), channel_id=1, source_target_pairs={{0,16},{8,24},{16,0},{24,8},{1,17},{9,25},{17,1},{25,9},{2,18},{10... | collective-permute-start | bytes 786440 | tf_op jit(solution)/shard_map/ppermute | solution.py:269
  28.6 10.3 %collective-permute-start.17 = (bf16[896,256]{1,0:T(8,128)(2,1)S(1)}, bf16[896,256]{1,0:T(8,128)(2,1)S(1)}, u32[]{:S(2)}, u32[]{:S(2)}) collective-permute-start(bf16[896,256]{1,0:T(8,128)(2,1)S(1)} %get-tuple-element.74.refs_0_), channel_id=1, source_target_pairs={{0,8},{8,0},{16,24},{24,16},{1,9},{9,1},{17,25},{25,17},{2,10},{10... | collective-permute-start | bytes 1376264 | tf_op jit(solution)/shard_map/ppermute | solution.py:269
  28.7 2.0 %collective-permute-start.14 = (bf16[2,4,2,16,256]{4,3,2,1,0:T(8,128)(2,1)S(1)}, bf16[2,4,2,16,256]{4,3,2,1,0:T(8,128)(2,1)S(1)}, u32[]{:S(2)}, u32[]{:S(2)}) collective-permute-start(bf16[2,4,2,16,256]{4,3,2,1,0:T(8,128)(2,1)S(1)} %get-tuple-element.68), channel_id=1, source_target_pairs={{0,8},{8,0},{16,24},{24,16},{1,9},{9,1},{17,25},{25,17},{2,10},{10... | collective-permute-start | bytes 393224 | tf_op jit(solution)/shard_map/ppermute | solution.py:269
  29.2 7.6 %collective-permute-start.16 = (bf16[384,256]{1,0:T(8,128)(2,1)S(1)}, bf16[384,256]{1,0:T(8,128)(2,1)S(1)}, u32[]{:S(2)}, u32[]{:S(2)}) collective-permute-start(bf16[384,256]{1,0:T(8,128)(2,1)S(1)} %get-tuple-element.66.refs_9_), channel_id=1, source_target_pairs={{0,16},{8,24},{16,0},{24,8},{1,17},{9,25},{17,1},{25,9},{2,18},{10... | collective-permute-start | bytes 589832 | tf_op jit(solution)/shard_map/ppermute | solution.py:269
  30.7 6.8 %collective-permute-start.15 = (bf16[1,4,2,16,256]{4,3,2,1,0:T(8,128)(2,1)S(1)}, bf16[1,4,2,16,256]{4,3,2,1,0:T(8,128)(2,1)S(1)}, u32[]{:S(2)}, u32[]{:S(2)}) collective-permute-start(bf16[1,4,2,16,256]{4,3,2,1,0:T(8,128)(2,1)S(1)} %get-tuple-element.71), channel_id=1, source_target_pairs={{0,16},{8,24},{16,0},{24,8},{1,17},{9,25},{17,1},{25,9},{2,18},{10... | collective-permute-start | bytes 196616 | tf_op jit(solution)/shard_map/ppermute | solution.py:269
  31.6 7.3 %collective-permute-start.18 = (bf16[512,256]{1,0:T(8,128)(2,1)S(1)}, bf16[512,256]{1,0:T(8,128)(2,1)S(1)}, u32[]{:S(2)}, u32[]{:S(2)}) collective-permute-start(bf16[512,256]{1,0:T(8,128)(2,1)S(1)} %collective-permute-done.10.refs_1_), channel_id=1, source_target_pairs={{0,8},{8,0},{16,24},{24,16},{1,9},{9,1},{17,25},{25,17},{2,10},{10... | collective-permute-start | bytes 786440 | tf_op jit(solution)/shard_map/ppermute | solution.py:269
  33.2 4.3 %copy-start = (bf16[1,128,256]{2,1,0:T(8,128)(2,1)S(1)}, bf16[1,128,256]{2,1,0:T(8,128)(2,1)}, u32[]{:S(2)}) copy-start(bf16[1,128,256]{2,1,0:T(8,128)(2,1)} %gate.1) | copy-start | bytes 196612
  33.2 4.3 %copy-start.1 = (bf16[1,128,256]{2,1,0:T(8,128)(2,1)S(1)}, bf16[1,128,256]{2,1,0:T(8,128)(2,1)}, u32[]{:S(2)}) copy-start(bf16[1,128,256]{2,1,0:T(8,128)(2,1)} %up.1) | copy-start | bytes 196612
  37.5 1.4 %collective-permute-start.19 = (bf16[384,256]{1,0:T(8,128)(2,1)S(1)}, bf16[384,256]{1,0:T(8,128)(2,1)S(1)}, u32[]{:S(2)}, u32[]{:S(2)}) collective-permute-start(bf16[384,256]{1,0:T(8,128)(2,1)S(1)} %collective-permute-done.16.refs_2_), channel_id=1, source_target_pairs={{0,8},{8,0},{16,24},{24,16},{1,9},{9,1},{17,25},{25,17},{2,10},{10... | collective-permute-start | bytes 589832 | tf_op jit(solution)/shard_map/ppermute | solution.py:269

commit v3 on v0

--- a/solution.py
+++ b/solution.py
@@ -61,11 +61,11 @@
                 (up_in, up),
                 (counts_in, counts),
                 (router_in, router),
-                (rows_in, rows),
             ]
+            + [(rows_in.at[0, f], rows.at[0, f]) for f in range(rows.shape[1])]
         )
     ]
-    for copy in copies:
+    for copy in copies[4:] + copies[:4]:
         copy.start()
     flight, slots, width = rows.shape[1:]
     pieces = cut.shape[0]
@@ -80,13 +80,14 @@
         for v in range(ways):
             at = (f * ways + v) * slots
             hidden[v, f] = value[at : at + slots]
-    for copy in copies[2:]:
-        copy.wait()
+    copies[2].wait()
+    copies[3].wait()
     diagonal = lax.broadcasted_iota(jnp.int32, (slots, slots), 0) == lax.broadcasted_iota(
         jnp.int32, (slots, slots), 1
     )
     row = lax.broadcasted_iota(jnp.int32, (slots, 1), 0)
     for f in range(flight):
+        copies[4 + f].wait()
         weight = jnp.sum(
             jnp.where(diagonal, jnp.broadcast_to(router[0, f : f + 1, :], (slots, slots)), 0.0),
             axis=1,
@@ -285,7 +286,7 @@
             pltpu.VMEM(gate_stash.shape, bf16),
             pltpu.VMEM(up_stash.shape, bf16),
             pltpu.VMEM((pieces, flight, slots, high), bf16),
-            pltpu.SemaphoreType.DMA((5,)),
+            pltpu.SemaphoreType.DMA((4 + flight,)),
         ],
         compiler_params=params(),
         name="scale",

time: 40.2 us -> 40.3 us (level)
  no operation moved by 1% of the time
where the time goes in v3:
time: 40.3 us; the launch traced here: 40.1 us
  starting transfers between devices  18.9 us (47%)
  waiting for transfers between devices  11.4 us (28%)
  Pallas kernels  9.02 us (22%)
  between operations  0.76 us (2%)
    ppermute x6, starting transfers between devices, local(): lax.ppermute(piece, 'expert', [(k, k ^ d) for k in range(sources)])  7.04 us
    ppermute x11, starting transfers between devices, over_dp(): return lax.ppermute(x, 'dp', [(i, i ^ d) for i in range(pieces)])  6.26 us
    ppermute x3, starting transfers between devices, local(): blocks[n] = lax.ppermute(blocks[n], ('dp', 'expert'), pairs)  5.64 us
    ppermute x11, waiting for transfers between devices, over_dp(): return lax.ppermute(x, 'dp', [(i, i ^ d) for i in range(pieces)])  4.71 us
    ppermute x6, waiting for transfers between devices, local(): lax.ppermute(piece, 'expert', [(k, k ^ d) for k in range(sources)])  3.63 us
    ppermute x3, waiting for transfers between devices, local(): blocks[n] = lax.ppermute(blocks[n], ('dp', 'expert'), pairs)  3.05 us
    pallas_call x2, Pallas kernels, join(): pl.pallas_call(functools.partial(join_kernel, high, [entry[:3] for entry...  1.9 us
    pallas_call x1, Pallas kernels, local(): pl.pallas_call(fetch_kernel, out_shape=[shape((high, across), f32)] * 3,...  1.76 us
  transfers between devices with their start and end apart: 20, of which 10 were waited for; matrix products, arithmetic and copies ran while one was open for 0% of the time, Pallas kernels for 17%

profile of v3, /device:TPU:0, one launch (start us, length us, event | category | flops | bytes accessed | tf_op | source)
XLA Modules:
  0.0 40.1 jit_solution(15728810015233223949)
XLA Ops:
  0.6 1.3 %scale.1 = (bf16[4,2,16,256]{3,2,1,0:T(8,128)(2,1)S(1)}, bf16[2,16,896]{2,1,0:T(8,128)(2,1)S(1)}, bf16[2,16,896]{2,1,0:T(8,128)(2,1)S(1)}, bf16[2,16,896]{2,1,0:T(8,128)(2,1)S(1)}, bf16[2,16,896]{2,1,0:T(8,128)(2,1)S(1)}) custom-call(s32[1,2]{1,0:T(1,128)} %counts_in.1, f32[1,2,16]{2,1,0:T(2,128)} %router_in.1, bf16[1,2,16,3584]{3,2,1,0:T(8,128)(2,1)} %rows_in.1, ...), custom_call_target="tpu_custom_call" | custom-call | tf_op jit(solution)/shard_map/scale/pallas_call | solution.py:276
  1.9 4.1 %collective-permute-start = (bf16[2,16,896]{2,1,0:T(8,128)(2,1)S(1)}, bf16[2,16,896]{2,1,0:T(8,128)(2,1)S(1)}, u32[]{:S(2)}, u32[]{:S(2)}) collective-permute-start(bf16[2,16,896]{2,1,0:T(8,128)(2,1)S(1)} %get-tuple-element.48), channel_id=1, source_target_pairs={{0,4},{1,5},{2,6},{3,7},{4,0},{5,1},{6,2},{7,3},{8,12},{9,13},{10,... | collective-permute-start | bytes 172040 | tf_op jit(solution)/shard_map/ppermute | solution.py:308
  6.0 1.3 %collective-permute-start.1 = (bf16[2,16,896]{2,1,0:T(8,128)(2,1)S(1)}, bf16[2,16,896]{2,1,0:T(8,128)(2,1)S(1)}, u32[]{:S(2)}, u32[]{:S(2)}) collective-permute-start(bf16[2,16,896]{2,1,0:T(8,128)(2,1)S(1)} %get-tuple-element.49), channel_id=1, source_target_pairs={{0,20},{1,21},{2,22},{3,23},{4,16},{5,17},{6,18},{7,19},{8,28},{9,... | collective-permute-start | bytes 172040 | tf_op jit(solution)/shard_map/ppermute | solution.py:308
  7.3 0.3 collective-permute-start.2
  7.6 1.8 %fetch.1 = (f32[896,256]{1,0:T(8,128)S(1)}, f32[896,256]{1,0:T(8,128)S(1)}, f32[896,256]{1,0:T(8,128)S(1)}) custom-call(bf16[4,2,16,256]{3,2,1,0:T(8,128)(2,1)S(1)} %get-tuple-element.52.after.refs_0_, f32[896,256]{1,0:T(8,128)} %refs_0_.1, f32[896,256]{1,0:T(8,128)} %refs_1_.1, f32[896,256]{1,0:T(8,128)} %refs_2_.1), custom_call_target="tpu_custom_call" | custom-call | bytes 5505024 | tf_op jit(solution)/shard_map/fetch/pallas_call | solution.py:309
  9.4 0.0 collective-permute-done.refs_0_.refs_2_
  9.4 3.0 %collective-permute-done.1.refs_1_.refs_3_ = bf16[2,16,896]{2,1,0:T(8,128)(2,1)S(1)} collective-permute-done((bf16[2,16,896]{2,1,0:T(8,128)(2,1)S(1)}, bf16[2,16,896]{2,1,0:T(8,128)(2,1)S(1)}, u32[]{:S(2)}, u32[]{:S(2)}) %collective-permute-start.1) | collective-permute-done | bytes 57376 | tf_op jit(solution)/shard_map/ppermute | solution.py:308
  12.4 0.0 collective-permute-done.2.refs_2_.refs_1_
  12.4 0.1 collective-permute-start.3
  12.5 1.4 %collective-permute-start.8 = (bf16[4,2,16,256]{3,2,1,0:T(8,128)(2,1)S(1)}, bf16[4,2,16,256]{3,2,1,0:T(8,128)(2,1)S(1)}, u32[]{:S(2)}, u32[]{:S(2)}) collective-permute-start(bf16[4,2,16,256]{3,2,1,0:T(8,128)(2,1)S(1)} %get-tuple-element.52.after.refs_0_), channel_id=1, source_target_pairs={{0,16},{8,24},{16,0},{24,8},{1,17},{9,25},{17,1},{25,9},{2,18},{10... | collective-permute-start | bytes 196616 | tf_op jit(solution)/shard_map/ppermute | solution.py:270
  13.9 0.0 collective-permute-done.3.other
  13.9 1.6 %collective-permute-start.6 = (bf16[8,16,512]{2,1,0:T(8,128)(2,1)S(1)}, bf16[8,16,512]{2,1,0:T(8,128)(2,1)S(1)}, u32[]{:S(2)}, u32[]{:S(2)}) collective-permute-start(bf16[8,16,512]{2,1,0:T(8,128)(2,1)S(1)} %get-tuple-element.60.refs_0_), channel_id=1, source_target_pairs={{0,1},{1,0},{2,3},{3,2},{4,5},{5,4},{6,7},{7,6},{8,9},{9,8},{10,11... | collective-permute-start | bytes 393224 | tf_op jit(solution)/shard_map/ppermute | solution.py:361
  15.5 1.4 %collective-permute-start.5 = (bf16[8,16,512]{2,1,0:T(8,128)(2,1)S(1)}, bf16[8,16,512]{2,1,0:T(8,128)(2,1)S(1)}, u32[]{:S(2)}, u32[]{:S(2)}) collective-permute-start(bf16[8,16,512]{2,1,0:T(8,128)(2,1)S(1)} %get-tuple-element.60.refs_0_), channel_id=1, source_target_pairs={{0,2},{1,3},{2,0},{3,1},{4,6},{5,7},{6,4},{7,5},{8,10},{9,11},{10,... | collective-permute-start | bytes 393224 | tf_op jit(solution)/shard_map/ppermute | solution.py:361
  16.9 0.6 %collective-permute-start.4 = (bf16[8,16,512]{2,1,0:T(8,128)(2,1)S(1)}, bf16[8,16,512]{2,1,0:T(8,128)(2,1)S(1)}, u32[]{:S(2)}, u32[]{:S(2)}) collective-permute-start(bf16[8,16,512]{2,1,0:T(8,128)(2,1)S(1)} %get-tuple-element.60.refs_0_), channel_id=1, source_target_pairs={{0,3},{1,2},{2,1},{3,0},{4,7},{5,6},{6,5},{7,4},{8,11},{9,10},{10,... | collective-permute-start | bytes 393224 | tf_op jit(solution)/shard_map/ppermute | solution.py:361
  17.5 0.0 collective-permute-start.7
  17.5 0.0 collective-permute-done.8.refs_2_
  17.5 0.5 %collective-permute-start.9 = (bf16[4,2,16,256]{3,2,1,0:T(8,128)(2,1)S(1)}, bf16[4,2,16,256]{3,2,1,0:T(8,128)(2,1)S(1)}, u32[]{:S(2)}, u32[]{:S(2)}) collective-permute-start(bf16[4,2,16,256]{3,2,1,0:T(8,128)(2,1)S(1)} %collective-permute-done.8.refs_2_), channel_id=1, source_target_pairs={{0,8},{8,0},{16,24},{24,16},{1,9},{9,1},{17,25},{25,17},{2,10},{10... | collective-permute-start | bytes 196616 | tf_op jit(solution)/shard_map/ppermute | solution.py:270
  18.0 0.7 %collective-permute-done.7.refs_1_ = bf16[4,2,16,256]{3,2,1,0:T(8,128)(2,1)S(1)} collective-permute-done((bf16[4,2,16,256]{3,2,1,0:T(8,128)(2,1)S(1)}, bf16[4,2,16,256]{3,2,1,0:T(8,128)(2,1)S(1)}, u32[]{:S(2)}, u32[]{:S(2)}) %collective-permute-start.7) | collective-permute-done | bytes 65568 | tf_op jit(solution)/shard_map/ppermute | solution.py:270
  18.7 1.5 %collective-permute-start.13 = (bf16[8,16,384]{2,1,0:T(8,128)(2,1)S(1)}, bf16[8,16,384]{2,1,0:T(8,128)(2,1)S(1)}, u32[]{:S(2)}, u32[]{:S(2)}) collective-permute-start(bf16[8,16,384]{2,1,0:T(8,128)(2,1)S(1)} %get-tuple-element.65.refs_0_.refs_4_), channel_id=1, source_target_pairs={{0,1},{1,0},{2,3},{3,2},{4,5},{5,4},{6,7},{7,6},{8,9},{9,8},{10,11... | collective-permute-start | bytes 294920 | tf_op jit(solution)/shard_map/ppermute | solution.py:361
  20.2 0.0 collective-permute-done.9.refs_3_
  20.3 1.4 %collective-permute-start.12 = (bf16[8,16,384]{2,1,0:T(8,128)(2,1)S(1)}, bf16[8,16,384]{2,1,0:T(8,128)(2,1)S(1)}, u32[]{:S(2)}, u32[]{:S(2)}) collective-permute-start(bf16[8,16,384]{2,1,0:T(8,128)(2,1)S(1)} %get-tuple-element.65.refs_0_.refs_4_), channel_id=1, source_target_pairs={{0,2},{1,3},{2,0},{3,1},{4,6},{5,7},{6,4},{7,5},{8,10},{9,11},{10,... | collective-permute-start | bytes 294920 | tf_op jit(solution)/shard_map/ppermute | solution.py:361
  21.6 0.0 collective-permute-done.6.refs_3_
  21.6 0.6 %collective-permute-start.11 = (bf16[8,16,384]{2,1,0:T(8,128)(2,1)S(1)}, bf16[8,16,384]{2,1,0:T(8,128)(2,1)S(1)}, u32[]{:S(2)}, u32[]{:S(2)}) collective-permute-start(bf16[8,16,384]{2,1,0:T(8,128)(2,1)S(1)} %get-tuple-element.65.refs_0_.refs_4_), channel_id=1, source_target_pairs={{0,3},{1,2},{2,1},{3,0},{4,7},{5,6},{6,5},{7,4},{8,11},{9,10},{10,... | collective-permute-start | bytes 294920 | tf_op jit(solution)/shard_map/ppermute | solution.py:361
  22.2 0.0 collective-permute-done.5.refs_2_
  22.3 2.1 %collective-permute-done.4.refs_1_ = bf16[8,16,512]{2,1,0:T(8,128)(2,1)S(1)} collective-permute-done((bf16[8,16,512]{2,1,0:T(8,128)(2,1)S(1)}, bf16[8,16,512]{2,1,0:T(8,128)(2,1)S(1)}, u32[]{:S(2)}, u32[]{:S(2)}) %collective-permute-start.4) | collective-permute-done | bytes 131104 | tf_op jit(solution)/shard_map/ppermute | solution.py:361
  24.4 0.7 %update.2 = (bf16[512,256]{1,0:T(8,128)(2,1)S(1)}, f32[512,256]{1,0:T(8,128)S(1)}, f32[512,256]{1,0:T(8,128)S(1)}, f32[512,256]{1,0:T(8,128)S(1)}) custom-call(bf16[8,16,512]{2,1,0:T(8,128)(2,1)S(1)} %get-tuple-element.60.refs_0_, bf16[8,16,512]{2,1,0:T(8,128)(2,1)S(1)} %collective-permute-done.4.refs_1_, ...), custom_call_target="tpu_custom_call" | custom-call | flops 134217728 | bytes 5963776 | tf_op jit(solution)/shard_map/update/pallas_call | solution.py:368
  25.1 1.2 %collective-permute-start.10 = (bf16[512,256]{1,0:T(8,128)(2,1)S(1)}, bf16[512,256]{1,0:T(8,128)(2,1)S(1)}, u32[]{:S(2)}, u32[]{:S(2)}) collective-permute-start(bf16[512,256]{1,0:T(8,128)(2,1)S(1)} %get-tuple-element.64.refs_8_), channel_id=1, source_target_pairs={{0,16},{8,24},{16,0},{24,8},{1,17},{9,25},{17,1},{25,9},{2,18},{10... | collective-permute-start | bytes 786440 | tf_op jit(solution)/shard_map/ppermute | solution.py:270
  26.3 0.1 collective-permute-done.13.refs_3_.refs_7_
  26.3 0.2 collective-permute-done.12.refs_2_.refs_6_
  26.5 1.3 %collective-permute-done.11.refs_1_.refs_5_ = bf16[8,16,384]{2,1,0:T(8,128)(2,1)S(1)} collective-permute-done((bf16[8,16,384]{2,1,0:T(8,128)(2,1)S(1)}, bf16[8,16,384]{2,1,0:T(8,128)(2,1)S(1)}, u32[]{:S(2)}, u32[]{:S(2)}) %collective-permute-start.11) | collective-permute-done | bytes 98336 | tf_op jit(solution)/shard_map/ppermute | solution.py:361
  27.8 0.6 %update.3 = (bf16[384,256]{1,0:T(8,128)(2,1)S(1)}, f32[384,256]{1,0:T(8,128)S(1)}, f32[384,256]{1,0:T(8,128)S(1)}, f32[384,256]{1,0:T(8,128)S(1)}) custom-call(bf16[8,16,384]{2,1,0:T(8,128)(2,1)S(1)} %get-tuple-element.65.refs_0_.refs_4_, bf16[8,16,384]{2,1,0:T(8,128)(2,1)S(1)} %collective-permute-done.11.refs_1_.refs_5_, ...), custom_call_target="tpu_custom_call" | custom-call | flops 100663296 | bytes 5963776 | tf_op jit(solution)/shard_map/update/pallas_call | solution.py:368
  28.4 0.4 %partial.1 = (f32[2,4,2,16,256]{4,3,2,1,0:T(8,128)S(1)}, bf16[2,4,2,16,256]{4,3,2,1,0:T(8,128)(2,1)S(1)}, bf16[896,256]{1,0:T(8,128)(2,1)S(1)}) custom-call(bf16[8,16,512]{2,1,0:T(8,128)(2,1)S(1)} %get-tuple-element.60.refs_0_, bf16[8,16,512]{2,1,0:T(8,128)(2,1)S(1)} %collective-permute-done.4.refs_1_, ...), custom_call_target="tpu_custom_call" | custom-call | flops 234881024 | bytes 2752512 | tf_op jit(solution)/shard_map/partial/pallas_call | solution.py:386
  28.8 0.1 collective-permute-start.17
  28.9 0.5 %collective-permute-start.14 = (bf16[2,4,2,16,256]{4,3,2,1,0:T(8,128)(2,1)S(1)}, bf16[2,4,2,16,256]{4,3,2,1,0:T(8,128)(2,1)S(1)}, u32[]{:S(2)}, u32[]{:S(2)}) collective-permute-start(bf16[2,4,2,16,256]{4,3,2,1,0:T(8,128)(2,1)S(1)} %get-tuple-element.68), channel_id=1, source_target_pairs={{0,8},{8,0},{16,24},{24,16},{1,9},{9,1},{17,25},{25,17},{2,10},{10... | collective-permute-start | bytes 393224 | tf_op jit(solution)/shard_map/ppermute | solution.py:270
  29.4 1.2 %collective-permute-start.16 = (bf16[384,256]{1,0:T(8,128)(2,1)S(1)}, bf16[384,256]{1,0:T(8,128)(2,1)S(1)}, u32[]{:S(2)}, u32[]{:S(2)}) collective-permute-start(bf16[384,256]{1,0:T(8,128)(2,1)S(1)} %get-tuple-element.66.refs_9_), channel_id=1, source_target_pairs={{0,16},{8,24},{16,0},{24,8},{1,17},{9,25},{17,1},{25,9},{2,18},{10... | collective-permute-start | bytes 589832 | tf_op jit(solution)/shard_map/ppermute | solution.py:270
  30.6 0.3 collective-permute-done.14.arrived
  30.9 1.3 %collective-permute-start.15 = (bf16[1,4,2,16,256]{4,3,2,1,0:T(8,128)(2,1)S(1)}, bf16[1,4,2,16,256]{4,3,2,1,0:T(8,128)(2,1)S(1)}, u32[]{:S(2)}, u32[]{:S(2)}) collective-permute-start(bf16[1,4,2,16,256]{4,3,2,1,0:T(8,128)(2,1)S(1)} %get-tuple-element.71), channel_id=1, source_target_pairs={{0,16},{8,24},{16,0},{24,8},{1,17},{9,25},{17,1},{25,9},{2,18},{10... | collective-permute-start | bytes 196616 | tf_op jit(solution)/shard_map/ppermute | solution.py:270
  32.2 0.0 collective-permute-done.10.refs_1_
  32.2 0.0 collective-permute-start.18
  32.2 1.6 %store.1 = (f32[896,256]{1,0:T(8,128)}, f32[896,256]{1,0:T(8,128)}, f32[896,256]{1,0:T(8,128)}) custom-call(f32[512,256]{1,0:T(8,128)S(1)} %get-tuple-element.76.refs_0_, f32[512,256]{1,0:T(8,128)S(1)} %get-tuple-element.77.refs_1_, f32[512,256]{1,0:T(8,128)S(1)} %get-tuple-element.78.refs_2_, f32[384,256]{1,0:T(8,128)S(1)} %get-tuple-element.79.refs_3_, ...), custom_call_target="tpu_custom_call" | custom-call | bytes 5505024 | tf_op jit(solution)/shard_map/store/pallas_call | solution.py:429
  33.8 0.0 copy-start
  33.8 0.0 copy-start.1
  33.8 0.9 %join.2.refs_4_ = bf16[3584,256]{1,0:T(8,128)(2,1)} custom-call(bf16[896,256]{1,0:T(8,128)(2,1)S(1)} %get-tuple-element.74.refs_0_, bf16[512,256]{1,0:T(8,128)(2,1)S(1)} %collective-permute-done.10.refs_1_), custom_call_target="tpu_custom_call" | custom-call | tf_op jit(solution)/shard_map/join/pallas_call | solution.py:441
  34.7 2.3 %collective-permute-done.16.refs_2_ = bf16[384,256]{1,0:T(8,128)(2,1)S(1)} collective-permute-done((bf16[384,256]{1,0:T(8,128)(2,1)S(1)}, bf16[384,256]{1,0:T(8,128)(2,1)S(1)}, u32[]{:S(2)}, u32[]{:S(2)}) %collective-permute-start.16) | collective-permute-done | bytes 196640 | tf_op jit(solution)/shard_map/ppermute | solution.py:270
  37.0 0.7 %collective-permute-done.15.arrived = bf16[1,4,2,16,256]{4,3,2,1,0:T(8,128)(2,1)S(1)} collective-permute-done((bf16[1,4,2,16,256]{4,3,2,1,0:T(8,128)(2,1)S(1)}, bf16[1,4,2,16,256]{4,3,2,1,0:T(8,128)(2,1)S(1)}, u32[]{:S(2)}, u32[]{:S(2)}) %collective-permute-start.15) | collective-permute-done | bytes 65568 | tf_op jit(solution)/shard_map/ppermute | solution.py:270
  37.7 0.0 collective-permute-start.19
  37.7 0.0 copy-done
  37.7 0.0 copy-done.1
  37.7 0.7 %gates.1 = (bf16[1,128,256]{2,1,0:T(8,128)(2,1)}, bf16[1,128,256]{2,1,0:T(8,128)(2,1)}) custom-call(bf16[1,128,256]{2,1,0:T(8,128)(2,1)S(1)} %copy-done, bf16[1,128,256]{2,1,0:T(8,128)(2,1)S(1)} %copy-done.1, f32[1,4,2,16,256]{4,3,2,1,0:T(8,128)S(1)} %get-tuple-element.70.held, bf16[1,4,2,16,256]{4,3,2,1,0:T(8,128)(2,1)S(1)} %collective-permute-done.15.arrived), custom_call_target="tpu_custom_call" | custom-call | tf_op jit(solution)/shard_map/gates/pallas_call | solution.py:420
  38.4 0.7 %collective-permute-done.19.refs_3_ = bf16[384,256]{1,0:T(8,128)(2,1)S(1)} collective-permute-done((bf16[384,256]{1,0:T(8,128)(2,1)S(1)}, bf16[384,256]{1,0:T(8,128)(2,1)S(1)}, u32[]{:S(2)}, u32[]{:S(2)}) %collective-permute-start.19) | collective-permute-done | bytes 196640 | tf_op jit(solution)/shard_map/ppermute | solution.py:270
  39.1 0.0 collective-permute-done.17.refs_0_
  39.1 0.0 collective-permute-done.18.refs_1_
  39.1 1.0 %join.3 = bf16[3584,256]{1,0:T(8,128)(2,1)} custom-call(bf16[896,256]{1,0:T(8,128)(2,1)S(1)} %collective-permute-done.17.refs_0_, bf16[512,256]{1,0:T(8,128)(2,1)S(1)} %collective-permute-done.18.refs_1_, bf16[384,256]{1,0:T(8,128)(2,1)S(1)} %collective-permute-done.16.refs_2_, ...), custom_call_target="tpu_custom_call", output_to_operand_aliasing={{}: (4, {})} | custom-call | tf_op jit(solution)/shard_map/join/pallas_call | solution.py:441
  (4 shorter events, 0.1 us)
Async XLA Ops:
  1.9 7.4 %collective-permute-start = (bf16[2,16,896]{2,1,0:T(8,128)(2,1)S(1)}, bf16[2,16,896]{2,1,0:T(8,128)(2,1)S(1)}, u32[]{:S(2)}, u32[]{:S(2)}) collective-permute-start(bf16[2,16,896]{2,1,0:T(8,128)(2,1)S(1)} %get-tuple-element.48), channel_id=1, source_target_pairs={{0,4},{1,5},{2,6},{3,7},{4,0},{5,1},{6,2},{7,3},{8,12},{9,13},{10,... | collective-permute-start | bytes 172040 | tf_op jit(solution)/shard_map/ppermute | solution.py:308
  6.0 6.4 %collective-permute-start.1 = (bf16[2,16,896]{2,1,0:T(8,128)(2,1)S(1)}, bf16[2,16,896]{2,1,0:T(8,128)(2,1)S(1)}, u32[]{:S(2)}, u32[]{:S(2)}) collective-permute-start(bf16[2,16,896]{2,1,0:T(8,128)(2,1)S(1)} %get-tuple-element.49), channel_id=1, source_target_pairs={{0,20},{1,21},{2,22},{3,23},{4,16},{5,17},{6,18},{7,19},{8,28},{9,... | collective-permute-start | bytes 172040 | tf_op jit(solution)/shard_map/ppermute | solution.py:308
  7.3 5.1 %collective-permute-start.2 = (bf16[2,16,896]{2,1,0:T(8,128)(2,1)S(1)}, bf16[2,16,896]{2,1,0:T(8,128)(2,1)S(1)}, u32[]{:S(2)}, u32[]{:S(2)}) collective-permute-start(bf16[2,16,896]{2,1,0:T(8,128)(2,1)S(1)} %get-tuple-element.50), channel_id=1, source_target_pairs={{0,16},{1,17},{2,18},{3,19},{4,20},{5,21},{6,22},{7,23},{8,24},{9,... | collective-permute-start | bytes 172040 | tf_op jit(solution)/shard_map/ppermute | solution.py:308
  12.4 1.5 %collective-permute-start.3 = (bf16[4,16,896]{2,1,0:T(8,128)(2,1)S(1)}, bf16[4,16,896]{2,1,0:T(8,128)(2,1)S(1)}, u32[]{:S(2)}, u32[]{:S(2)}) collective-permute-start(bf16[4,16,896]{2,1,0:T(8,128)(2,1)S(1)} %share.1), channel_id=1, source_target_pairs={{0,8},{8,0},{16,24},{24,16},{1,9},{9,1},{17,25},{25,17},{2,10},{10... | collective-permute-start | bytes 344072 | tf_op jit(solution)/shard_map/ppermute | solution.py:270
  12.5 5.0 %collective-permute-start.8 = (bf16[4,2,16,256]{3,2,1,0:T(8,128)(2,1)S(1)}, bf16[4,2,16,256]{3,2,1,0:T(8,128)(2,1)S(1)}, u32[]{:S(2)}, u32[]{:S(2)}) collective-permute-start(bf16[4,2,16,256]{3,2,1,0:T(8,128)(2,1)S(1)} %get-tuple-element.52.after.refs_0_), channel_id=1, source_target_pairs={{0,16},{8,24},{16,0},{24,8},{1,17},{9,25},{17,1},{25,9},{2,18},{10... | collective-permute-start | bytes 196616 | tf_op jit(solution)/shard_map/ppermute | solution.py:270
  13.9 7.7 %collective-permute-start.6 = (bf16[8,16,512]{2,1,0:T(8,128)(2,1)S(1)}, bf16[8,16,512]{2,1,0:T(8,128)(2,1)S(1)}, u32[]{:S(2)}, u32[]{:S(2)}) collective-permute-start(bf16[8,16,512]{2,1,0:T(8,128)(2,1)S(1)} %get-tuple-element.60.refs_0_), channel_id=1, source_target_pairs={{0,1},{1,0},{2,3},{3,2},{4,5},{5,4},{6,7},{7,6},{8,9},{9,8},{10,11... | collective-permute-start | bytes 393224 | tf_op jit(solution)/shard_map/ppermute | solution.py:361
  15.5 6.7 %collective-permute-start.5 = (bf16[8,16,512]{2,1,0:T(8,128)(2,1)S(1)}, bf16[8,16,512]{2,1,0:T(8,128)(2,1)S(1)}, u32[]{:S(2)}, u32[]{:S(2)}) collective-permute-start(bf16[8,16,512]{2,1,0:T(8,128)(2,1)S(1)} %get-tuple-element.60.refs_0_), channel_id=1, source_target_pairs={{0,2},{1,3},{2,0},{3,1},{4,6},{5,7},{6,4},{7,5},{8,10},{9,11},{10,... | collective-permute-start | bytes 393224 | tf_op jit(solution)/shard_map/ppermute | solution.py:361
  16.9 7.5 %collective-permute-start.4 = (bf16[8,16,512]{2,1,0:T(8,128)(2,1)S(1)}, bf16[8,16,512]{2,1,0:T(8,128)(2,1)S(1)}, u32[]{:S(2)}, u32[]{:S(2)}) collective-permute-start(bf16[8,16,512]{2,1,0:T(8,128)(2,1)S(1)} %get-tuple-element.60.refs_0_), channel_id=1, source_target_pairs={{0,3},{1,2},{2,1},{3,0},{4,7},{5,6},{6,5},{7,4},{8,11},{9,10},{10,... | collective-permute-start | bytes 393224 | tf_op jit(solution)/shard_map/ppermute | solution.py:361
  17.5 1.3 %collective-permute-start.7 = (bf16[4,2,16,256]{3,2,1,0:T(8,128)(2,1)S(1)}, bf16[4,2,16,256]{3,2,1,0:T(8,128)(2,1)S(1)}, u32[]{:S(2)}, u32[]{:S(2)}) collective-permute-start(bf16[4,2,16,256]{3,2,1,0:T(8,128)(2,1)S(1)} %get-tuple-element.52.after.refs_0_), channel_id=1, source_target_pairs={{0,8},{8,0},{16,24},{24,16},{1,9},{9,1},{17,25},{25,17},{2,10},{10... | collective-permute-start | bytes 196616 | tf_op jit(solution)/shard_map/ppermute | solution.py:270
  17.5 2.8 %collective-permute-start.9 = (bf16[4,2,16,256]{3,2,1,0:T(8,128)(2,1)S(1)}, bf16[4,2,16,256]{3,2,1,0:T(8,128)(2,1)S(1)}, u32[]{:S(2)}, u32[]{:S(2)}) collective-permute-start(bf16[4,2,16,256]{3,2,1,0:T(8,128)(2,1)S(1)} %collective-permute-done.8.refs_2_), channel_id=1, source_target_pairs={{0,8},{8,0},{16,24},{24,16},{1,9},{9,1},{17,25},{25,17},{2,10},{10... | collective-permute-start | bytes 196616 | tf_op jit(solution)/shard_map/ppermute | solution.py:270
  18.7 7.6 %collective-permute-start.13 = (bf16[8,16,384]{2,1,0:T(8,128)(2,1)S(1)}, bf16[8,16,384]{2,1,0:T(8,128)(2,1)S(1)}, u32[]{:S(2)}, u32[]{:S(2)}) collective-permute-start(bf16[8,16,384]{2,1,0:T(8,128)(2,1)S(1)} %get-tuple-element.65.refs_0_.refs_4_), channel_id=1, source_target_pairs={{0,1},{1,0},{2,3},{3,2},{4,5},{5,4},{6,7},{7,6},{8,9},{9,8},{10,11... | collective-permute-start | bytes 294920 | tf_op jit(solution)/shard_map/ppermute | solution.py:361
  20.3 6.3 %collective-permute-start.12 = (bf16[8,16,384]{2,1,0:T(8,128)(2,1)S(1)}, bf16[8,16,384]{2,1,0:T(8,128)(2,1)S(1)}, u32[]{:S(2)}, u32[]{:S(2)}) collective-permute-start(bf16[8,16,384]{2,1,0:T(8,128)(2,1)S(1)} %get-tuple-element.65.refs_0_.refs_4_), channel_id=1, source_target_pairs={{0,2},{1,3},{2,0},{3,1},{4,6},{5,7},{6,4},{7,5},{8,10},{9,11},{10,... | collective-permute-start | bytes 294920 | tf_op jit(solution)/shard_map/ppermute | solution.py:361
  21.6 6.2 %collective-permute-start.11 = (bf16[8,16,384]{2,1,0:T(8,128)(2,1)S(1)}, bf16[8,16,384]{2,1,0:T(8,128)(2,1)S(1)}, u32[]{:S(2)}, u32[]{:S(2)}) collective-permute-start(bf16[8,16,384]{2,1,0:T(8,128)(2,1)S(1)} %get-tuple-element.65.refs_0_.refs_4_), channel_id=1, source_target_pairs={{0,3},{1,2},{2,1},{3,0},{4,7},{5,6},{6,5},{7,4},{8,11},{9,10},{10,... | collective-permute-start | bytes 294920 | tf_op jit(solution)/shard_map/ppermute | solution.py:361
  25.1 7.1 %collective-permute-start.10 = (bf16[512,256]{1,0:T(8,128)(2,1)S(1)}, bf16[512,256]{1,0:T(8,128)(2,1)S(1)}, u32[]{:S(2)}, u32[]{:S(2)}) collective-permute-start(bf16[512,256]{1,0:T(8,128)(2,1)S(1)} %get-tuple-element.64.refs_8_), channel_id=1, source_target_pairs={{0,16},{8,24},{16,0},{24,8},{1,17},{9,25},{17,1},{25,9},{2,18},{10... | collective-permute-start | bytes 786440 | tf_op jit(solution)/shard_map/ppermute | solution.py:270
  28.8 10.3 %collective-permute-start.17 = (bf16[896,256]{1,0:T(8,128)(2,1)S(1)}, bf16[896,256]{1,0:T(8,128)(2,1)S(1)}, u32[]{:S(2)}, u32[]{:S(2)}) collective-permute-start(bf16[896,256]{1,0:T(8,128)(2,1)S(1)} %get-tuple-element.74.refs_0_), channel_id=1, source_target_pairs={{0,8},{8,0},{16,24},{24,16},{1,9},{9,1},{17,25},{25,17},{2,10},{10... | collective-permute-start | bytes 1376264 | tf_op jit(solution)/shard_map/ppermute | solution.py:270
  28.9 2.0 %collective-permute-start.14 = (bf16[2,4,2,16,256]{4,3,2,1,0:T(8,128)(2,1)S(1)}, bf16[2,4,2,16,256]{4,3,2,1,0:T(8,128)(2,1)S(1)}, u32[]{:S(2)}, u32[]{:S(2)}) collective-permute-start(bf16[2,4,2,16,256]{4,3,2,1,0:T(8,128)(2,1)S(1)} %get-tuple-element.68), channel_id=1, source_target_pairs={{0,8},{8,0},{16,24},{24,16},{1,9},{9,1},{17,25},{25,17},{2,10},{10... | collective-permute-start | bytes 393224 | tf_op jit(solution)/shard_map/ppermute | solution.py:270
  29.4 7.6 %collective-permute-start.16 = (bf16[384,256]{1,0:T(8,128)(2,1)S(1)}, bf16[384,256]{1,0:T(8,128)(2,1)S(1)}, u32[]{:S(2)}, u32[]{:S(2)}) collective-permute-start(bf16[384,256]{1,0:T(8,128)(2,1)S(1)} %get-tuple-element.66.refs_9_), channel_id=1, source_target_pairs={{0,16},{8,24},{16,0},{24,8},{1,17},{9,25},{17,1},{25,9},{2,18},{10... | collective-permute-start | bytes 589832 | tf_op jit(solution)/shard_map/ppermute | solution.py:270
  30.9 6.8 %collective-permute-start.15 = (bf16[1,4,2,16,256]{4,3,2,1,0:T(8,128)(2,1)S(1)}, bf16[1,4,2,16,256]{4,3,2,1,0:T(8,128)(2,1)S(1)}, u32[]{:S(2)}, u32[]{:S(2)}) collective-permute-start(bf16[1,4,2,16,256]{4,3,2,1,0:T(8,128)(2,1)S(1)} %get-tuple-element.71), channel_id=1, source_target_pairs={{0,16},{8,24},{16,0},{24,8},{1,17},{9,25},{17,1},{25,9},{2,18},{10... | collective-permute-start | bytes 196616 | tf_op jit(solution)/shard_map/ppermute | solution.py:270
  32.2 6.9 %collective-permute-start.18 = (bf16[512,256]{1,0:T(8,128)(2,1)S(1)}, bf16[512,256]{1,0:T(8,128)(2,1)S(1)}, u32[]{:S(2)}, u32[]{:S(2)}) collective-permute-start(bf16[512,256]{1,0:T(8,128)(2,1)S(1)} %collective-permute-done.10.refs_1_), channel_id=1, source_target_pairs={{0,8},{8,0},{16,24},{24,16},{1,9},{9,1},{17,25},{25,17},{2,10},{10... | collective-permute-start | bytes 786440 | tf_op jit(solution)/shard_map/ppermute | solution.py:270
  33.8 3.9 %copy-start = (bf16[1,128,256]{2,1,0:T(8,128)(2,1)S(1)}, bf16[1,128,256]{2,1,0:T(8,128)(2,1)}, u32[]{:S(2)}) copy-start(bf16[1,128,256]{2,1,0:T(8,128)(2,1)} %gate.1) | copy-start | bytes 196612
  33.8 3.9 %copy-start.1 = (bf16[1,128,256]{2,1,0:T(8,128)(2,1)S(1)}, bf16[1,128,256]{2,1,0:T(8,128)(2,1)}, u32[]{:S(2)}) copy-start(bf16[1,128,256]{2,1,0:T(8,128)(2,1)} %up.1) | copy-start | bytes 196612
  37.7 1.4 %collective-permute-start.19 = (bf16[384,256]{1,0:T(8,128)(2,1)S(1)}, bf16[384,256]{1,0:T(8,128)(2,1)S(1)}, u32[]{:S(2)}, u32[]{:S(2)}) collective-permute-start(bf16[384,256]{1,0:T(8,128)(2,1)S(1)} %collective-permute-done.16.refs_2_), channel_id=1, source_target_pairs={{0,8},{8,0},{16,24},{24,16},{1,9},{9,1},{17,25},{25,17},{2,10},{10... | collective-permute-start | bytes 589832 | tf_op jit(solution)/shard_map/ppermute | solution.py:270
